TPU v7x, 32 devices: a whole 2x2x4 slice. The times are simulated.
32 devices in a mesh: dp: 16 (over z, y, core), ctx: 2 (over x).
Axes of the slice: x: 2, y: 2, z: 4, core: 2. Of those that a mesh axis runs over, the one named last changes fastest.
Arguments:
- tokens: bfloat16 [48, 1024, 768], P('dp', 'ctx'), may hold values from -6 to 6
- segments: int32 [48, 1024], P('dp'), may hold values from 0 to 3, as said below
- qkv_weight: bfloat16 [768, 2304], P(('dp', 'ctx')), may hold values from -0.21875 to 0.21875
- out_weight: bfloat16 [768, 768], P(('dp', 'ctx')), may hold values from -1.75 to 1.75
- up_weight: bfloat16 [768, 3072], P(('dp', 'ctx')), may hold values from -0.21875 to 0.21875
- down_weight: bfloat16 [3072, 768], P(('dp', 'ctx')), may hold values from -0.109375 to 0.109375
- vectors: bfloat16 [8, 768], P(None, ('dp', 'ctx')), may hold values from -2 to 2
- up_bias: bfloat16 [3072], P(('dp', 'ctx')), may hold values from -4 to 4
- cotangent: bfloat16 [48, 1024, 768], P('dp', 'ctx'), may hold values from -6 to 6
Outputs:
- block_out: bfloat16 [48, 1024, 768], P('dp', 'ctx')
- input_grad: float32 [48, 1024, 768], P('dp', 'ctx')
- qkv_grad: float32 [768, 2304], P(('dp', 'ctx'))
- out_grad: float32 [768, 768], P(('dp', 'ctx'))
- up_grad: float32 [768, 3072], P(('dp', 'ctx'))
- down_grad: float32 [3072, 768], P(('dp', 'ctx'))
- vector_grad: float32 [8, 768], P(None, ('dp', 'ctx'))
- up_bias_grad: float32 [3072], P(('dp', 'ctx'))
Inputs may be any that keep to these rules, and one draw needn't show every extreme that they name: segments never fall along a sequence, start at 0 and end at 3.
All inputs are finite; a program needn't handle non-finite values.
Results may differ from a plain program's by a relative error of at most 0.01.
Values may be sent and summed in bfloat16 or wider, within the bound.
A program may use at most 320 MiB of HBM per device.

v0:
```python
import jax
import jax.numpy as jnp
from jax import lax
from jax.sharding import PartitionSpec as P

HEADS = 12


EPSILON = 1e-05


def layer_norm(values, norm_gain, norm_shift):
    average = jnp.mean(values, -1, keepdims=True)
    centred = values - average
    variance = jnp.mean(centred * centred, -1, keepdims=True)
    return centred * lax.rsqrt(variance + EPSILON) * norm_gain + norm_shift


def gelu_tanh(pre_act):
    return jax.nn.gelu(pre_act, approximate=True)


def contract_rows(left, right):
    return lax.dot_general(
        left, right, (((0,), (0,)), ((), ())), preferred_element_type=jnp.float32
    )


def contract_cols(left, right):
    return lax.dot_general(
        left, right, (((1,), (1,)), ((), ())), preferred_element_type=jnp.float32
    )


def soft_probs(query_heads, key_heads, allowed, factor):
    scores = (
        jnp.einsum("qhd,khd->hqk", query_heads, key_heads, preferred_element_type=jnp.float32)
        * factor
    )
    scores = jnp.where(allowed[None], scores, -1e30)
    top_score = jnp.max(scores, -1, keepdims=True)
    expo = jnp.exp(scores - top_score)
    total = jnp.sum(expo, -1, keepdims=True)
    return (expo / total, top_score, total)


def on_device(
    tokens, segments, qkv_weight, out_weight, up_weight, down_weight, vectors, up_bias, cotangent
):
    micro_count, span_rows, model_width = tokens.shape
    head_dim = model_width // HEADS
    seq_length = segments.shape[1]
    hidden_units = up_weight.shape[1]
    factor = head_dim ** (-0.5)
    shards = (qkv_weight, out_weight, up_weight, down_weight, vectors, up_bias)
    q_start = lax.axis_index("ctx") * span_rows
    q_place = q_start + jnp.arange(span_rows, dtype=jnp.int32)
    k_place = jnp.arange(seq_length, dtype=jnp.int32)
    grad_qkv = jnp.zeros((model_width, 3 * model_width), jnp.float32)
    grad_out = jnp.zeros((model_width, model_width), jnp.float32)
    grad_up = jnp.zeros((model_width, hidden_units), jnp.float32)
    grad_down = jnp.zeros((hidden_units, model_width), jnp.float32)
    grad_vec = jnp.zeros((8, model_width), jnp.float32)
    grad_bias = jnp.zeros((hidden_units,), jnp.float32)
    outputs = []
    input_grads = []
    for micro_step in range(micro_count):
        forward_w = (
            lax.all_gather(shards[0], ("dp", "ctx"), axis=0, tiled=True),
            lax.all_gather(shards[1], ("dp", "ctx"), axis=0, tiled=True),
            lax.all_gather(shards[2], ("dp", "ctx"), axis=0, tiled=True),
            lax.all_gather(shards[3], ("dp", "ctx"), axis=0, tiled=True),
            lax.all_gather(shards[4], ("dp", "ctx"), axis=1, tiled=True),
            lax.all_gather(shards[5], ("dp", "ctx"), axis=0, tiled=True),
        )
        w_qkv, w_out, w_up, w_down, vec_all, bias_all = forward_w
        vec_rows = vec_all.astype(jnp.float32)
        token_rows = tokens[micro_step].astype(jnp.float32)
        seq_segs = segments[micro_step]
        own_segs = lax.dynamic_slice_in_dim(seq_segs, q_start, span_rows)
        allowed = (k_place[None, :] <= q_place[:, None]) & (seq_segs[None, :] == own_segs[:, None])
        hidden = layer_norm(token_rows, vec_rows[0], vec_rows[1]).astype(jnp.bfloat16)
        mixed = jnp.dot(hidden, w_qkv, preferred_element_type=jnp.float32)
        query_low = (mixed[:, :model_width] + vec_rows[2]).astype(jnp.bfloat16)
        key_low = mixed[:, model_width : 2 * model_width].astype(jnp.bfloat16)
        value_low = (mixed[:, 2 * model_width :] + vec_rows[3]).astype(jnp.bfloat16)
        key_all, value_all = (
            lax.all_gather(key_low, "ctx", axis=0, tiled=True),
            lax.all_gather(value_low, "ctx", axis=0, tiled=True),
        )
        query_heads = query_low.reshape(span_rows, HEADS, head_dim)
        key_heads = key_all.reshape(seq_length, HEADS, head_dim)
        value_heads = value_all.reshape(seq_length, HEADS, head_dim)
        probs = soft_probs(query_heads, key_heads, allowed, factor)[0]
        probs_low = probs.astype(jnp.bfloat16)
        attended = jnp.einsum(
            "hqk,khd->qhd", probs_low, value_heads, preferred_element_type=jnp.float32
        )
        attended = attended.reshape(span_rows, model_width).astype(jnp.bfloat16)
        middle = (
            token_rows + jnp.dot(attended, w_out, preferred_element_type=jnp.float32) + vec_rows[4]
        )
        inner = layer_norm(middle, vec_rows[5], vec_rows[6]).astype(jnp.bfloat16)
        pre_act = jnp.dot(inner, w_up, preferred_element_type=jnp.float32) + bias_all.astype(
            jnp.float32
        )
        active = gelu_tanh(pre_act).astype(jnp.bfloat16)
        result = middle + jnp.dot(active, w_down, preferred_element_type=jnp.float32) + vec_rows[7]
        outputs.append(result.astype(jnp.bfloat16))
        backward_w = (
            lax.all_gather(shards[0], ("dp", "ctx"), axis=0, tiled=True),
            lax.all_gather(shards[1], ("dp", "ctx"), axis=0, tiled=True),
            lax.all_gather(shards[2], ("dp", "ctx"), axis=0, tiled=True),
            lax.all_gather(shards[3], ("dp", "ctx"), axis=0, tiled=True),
            lax.all_gather(shards[4], ("dp", "ctx"), axis=1, tiled=True),
            lax.all_gather(shards[5], ("dp", "ctx"), axis=0, tiled=True),
        )
        b_qkv, b_out, b_up, b_down, unused_vec, unused_bias = backward_w
        grad_low = cotangent[micro_step]
        grad_rows = grad_low.astype(jnp.float32)
        grad_down = grad_down + contract_rows(active, grad_low)
        grad_bdown = jnp.sum(grad_rows, 0)
        grad_act = contract_cols(grad_low, b_down)
        unused_out, gelu_back = jax.vjp(gelu_tanh, pre_act)
        grad_pre = gelu_back(grad_act)[0].astype(jnp.bfloat16)
        grad_up = grad_up + contract_rows(inner, grad_pre)
        grad_bias = grad_bias + jnp.sum(grad_pre.astype(jnp.float32), 0)
        grad_inner = contract_cols(grad_pre, b_up)
        unused_norm, norm_two_back = jax.vjp(layer_norm, middle, vec_rows[5], vec_rows[6])
        grad_mid_norm, grad_gain_two, grad_shift_two = norm_two_back(grad_inner)
        grad_middle = grad_rows + grad_mid_norm
        grad_branch = grad_middle.astype(jnp.bfloat16)
        grad_out = grad_out + contract_rows(attended, grad_branch)
        grad_bout = jnp.sum(grad_branch.astype(jnp.float32), 0)
        grad_att = contract_cols(grad_branch, b_out).astype(jnp.bfloat16)
        grad_att_heads = grad_att.reshape(span_rows, HEADS, head_dim)
        probs, top_score, total = soft_probs(query_heads, key_heads, allowed, factor)
        probs_low = probs.astype(jnp.bfloat16)
        grad_probs = jnp.einsum(
            "qhd,khd->hqk", grad_att_heads, value_heads, preferred_element_type=jnp.float32
        )
        row_dot = jnp.sum(probs * grad_probs, -1, keepdims=True)
        grad_scores = (probs * (grad_probs - row_dot)).astype(jnp.bfloat16)
        grad_query = (
            jnp.einsum("hqk,khd->qhd", grad_scores, key_heads, preferred_element_type=jnp.float32)
            * factor
        )
        grad_query = grad_query.reshape(span_rows, model_width).astype(jnp.bfloat16)
        grad_keys = (
            jnp.einsum("hqk,qhd->khd", grad_scores, query_heads, preferred_element_type=jnp.float32)
            * factor
        )
        grad_values = jnp.einsum(
            "hqk,qhd->khd", probs_low, grad_att_heads, preferred_element_type=jnp.float32
        )
        kv_terms = jnp.concatenate(
            [
                grad_keys.reshape(seq_length, model_width),
                grad_values.reshape(seq_length, model_width),
            ],
            1,
        )
        own_kv = lax.psum_scatter(
            kv_terms.astype(jnp.bfloat16), "ctx", scatter_dimension=0, tiled=True
        ).astype(jnp.float32)
        grad_key_low = own_kv[:, :model_width].astype(jnp.bfloat16)
        grad_value_low = own_kv[:, model_width:].astype(jnp.bfloat16)
        grad_mixed = jnp.concatenate([grad_query, grad_key_low, grad_value_low], 1)
        grad_qkv = grad_qkv + contract_rows(hidden, grad_mixed)
        grad_bquery = jnp.sum(grad_query.astype(jnp.float32), 0)
        grad_bvalue = jnp.sum(grad_value_low.astype(jnp.float32), 0)
        grad_hidden = contract_cols(grad_mixed, b_qkv)
        unused_first, norm_one_back = jax.vjp(layer_norm, token_rows, vec_rows[0], vec_rows[1])
        grad_tok_norm, grad_gain_one, grad_shift_one = norm_one_back(grad_hidden)
        input_grads.append(grad_middle + grad_tok_norm)
        grad_vec = grad_vec + jnp.stack(
            [
                grad_gain_one,
                grad_shift_one,
                grad_bquery,
                grad_bvalue,
                grad_bout,
                grad_gain_two,
                grad_shift_two,
                grad_bdown,
            ]
        )
    owned = (
        lax.psum_scatter(grad_qkv, ("dp", "ctx"), scatter_dimension=0, tiled=True),
        lax.psum_scatter(grad_out, ("dp", "ctx"), scatter_dimension=0, tiled=True),
        lax.psum_scatter(grad_up, ("dp", "ctx"), scatter_dimension=0, tiled=True),
        lax.psum_scatter(grad_down, ("dp", "ctx"), scatter_dimension=0, tiled=True),
        lax.psum_scatter(grad_vec, ("dp", "ctx"), scatter_dimension=1, tiled=True),
        lax.psum_scatter(grad_bias, ("dp", "ctx"), scatter_dimension=0, tiled=True),
    )
    return (
        jnp.stack(outputs),
        jnp.stack(input_grads),
        owned[0],
        owned[1],
        owned[2],
        owned[3],
        owned[4],
        owned[5],
    )


def solution(mesh):
    placed = (
        P("dp", "ctx", None),
        P("dp", None),
        P(("dp", "ctx"), None),
        P(("dp", "ctx"), None),
        P(("dp", "ctx"), None),
        P(("dp", "ctx"), None),
        P(None, ("dp", "ctx")),
        P(("dp", "ctx")),
        P("dp", "ctx", None),
    )
    return jax.shard_map(
        on_device,
        mesh=mesh,
        in_specs=placed,
        out_specs=(
            P("dp", "ctx", None),
            P("dp", "ctx", None),
            P(("dp", "ctx"), None),
            P(("dp", "ctx"), None),
            P(("dp", "ctx"), None),
            P(("dp", "ctx"), None),
            P(None, ("dp", "ctx")),
            P(("dp", "ctx")),
        ),
        check_vma=False,
    )
```

profile of v0, /device:TPU:0, one launch (start us, length us, event | category | flops | bytes accessed | tf_op | source)
XLA Modules:
  0.0 1307.9 jit_solution(11375473477013354423)
XLA Ops:
  8.0 70.7 %all-gather = bf16[32,24,8]{1,2,0:T(8,128)(2,1)S(1)} all-gather(bf16[1,24,8]{1,2,0:T(8,128)(2,1)} %bitcast.354), channel_id=1, replica_groups=mesh['dp'=16,'ctx'=2] {'dp','ctx'}, dimensions={0}, use_global_device_ids=true | all-gather | bytes 12672 | tf_op jit(solution)/shard_map/all_gather | solution.py:73
  103.4 37.6 %all-reduce = bf16[3072]{0:T(1024)(128)(2,1)S(1)} all-reduce(bf16[3072]{0:T(1024)(128)(2,1)S(1)} %dynamic-update-slice), channel_id=1, replica_groups=mesh['dp'=16,'ctx'=2] {'dp','ctx'}, use_global_device_ids=true, to_apply=%add | all-reduce | flops 3072 | bytes 12288
  149.9 14.5 %fusion.201 = (f32[12,512]{1,0:T(8,128)S(1)}, f32[12,512,1024]{2,1,0:T(8,128)}) fusion(pred[512,1024]{1,0:T(8,128)(4,1)} %get-tuple-element.88, bf16[512,12,64]{0,2,1:T(8,128)(2,1)S(1)} %bitcast.314, bf16[1024,12,64]{0,2,1:T(8,128)(2,1)} %bitcast.308), kind=kOutput, calls=%fused_computation.313 | convolution fusion | flops 830473216 | bytes 28073984 | tf_op jit(solution)/shard_map/sub | solution.py:42
  167.0 5.9 all-gather.30.cloned.1.call-done
  175.5 26.1 %all-gather.28.cloned.1.call-done = bf16[1024,768]{1,0:T(8,128)(2,1)} async-done(((bf16[512,768]{1,0:T(8,128)(2,1)}), bf16[1024,768]{1,0:T(8,128)(2,1)}) %all-gather.28.cloned.1.call-update) | async-done | bytes 1572880 | tf_op jit(solution)/shard_map/all_gather | solution.py:89
  204.1 11.7 fusion.116
  215.8 42.7 %all-gather.18.cloned.1.call-done = bf16[768,768]{1,0:T(8,128)(2,1)} async-done(((bf16[24,768]{1,0:T(8,128)(2,1)}), bf16[768,768]{1,0:T(8,128)(2,1)}) %all-gather.18.cloned.1.call-update) | async-done | bytes 1179664 | tf_op jit(solution)/shard_map/all_gather | solution.py:70
  262.5 14.9 %fusion.199 = (f32[12,512]{1,0:T(8,128)S(1)}, f32[12,512,1024]{2,1,0:T(8,128)}) fusion(pred[512,1024]{1,0:T(8,128)(4,1)} %get-tuple-element.87, bf16[512,12,64]{0,2,1:T(8,128)(2,1)S(1)} %bitcast.316, bf16[1024,12,64]{0,2,1:T(8,128)(2,1)} %bitcast.310), kind=kOutput, calls=%fused_computation.311 | convolution fusion | flops 830473216 | bytes 28073984 | tf_op jit(solution)/shard_map/sub | solution.py:42
  277.4 10.9 fusion.119
  290.7 33.3 %all-gather.20.cloned.1.call-done = bf16[768,3072]{1,0:T(8,128)(2,1)} async-done(((bf16[24,3072]{1,0:T(8,128)(2,1)}), bf16[768,3072]{1,0:T(8,128)(2,1)}) %all-gather.20.cloned.1.call-update) | async-done | bytes 4718608 | tf_op jit(solution)/shard_map/all_gather | solution.py:71
  324.0 8.2 fusion.190
  332.3 57.1 %all-gather.22.cloned.1.call-done = bf16[3072,768]{1,0:T(8,128)(2,1)} async-done(((bf16[96,768]{1,0:T(8,128)(2,1)}), bf16[3072,768]{1,0:T(8,128)(2,1)}) %all-gather.22.cloned.1.call-update) | async-done | bytes 4718608 | tf_op jit(solution)/shard_map/all_gather | solution.py:72
  389.4 9.9 convert_reduce_fusion.1
  404.9 7.1 convert_reduce_fusion
  422.9 19.2 %multiply_reduce_fusion = (f32[12,512]{1,0:T(8,128)S(1)}, f32[12,512,1024]{2,1,0:T(8,128)}) fusion(f32[12,512,1024]{2,1,0:T(8,128)} %get-tuple-element.90, f32[12,512]{1,0:T(8,128)S(1)} %get-tuple-element.89, bf16[512,12,64]{0,2,1:T(8,128)(2,1)S(1)} %bitcast.339, bf16[1024,12,64]{0,2,1:T(8,128)(2,1)S(1)} %bitcast.325), kind=kOutput, calls=%fused_computation.4 | convolution fusion | flops 824174592 | bytes 52740096 | tf_op jit(solution)/shard_map/qhd,khd->hqk/dot_general | solution.py:139
  442.0 11.1 fusion.81
  456.2 18.9 %multiply_reduce_fusion.1 = (f32[12,512]{1,0:T(8,128)S(1)}, f32[12,512,1024]{2,1,0:T(8,128)}) fusion(f32[12,512,1024]{2,1,0:T(8,128)} %get-tuple-element.94, f32[12,512]{1,0:T(8,128)S(1)} %copy-done.73, bf16[512,12,64]{0,2,1:T(8,128)(2,1)S(1)} %bitcast.337, bf16[1024,12,64]{0,2,1:T(8,128)(2,1)S(1)} %bitcast.323), kind=kOutput, calls=%fused_computation.6 | convolution fusion | flops 824174592 | bytes 52740096 | tf_op jit(solution)/shard_map/qhd,khd->hqk/dot_general | solution.py:139
  475.1 16.3 %multiply_convert_fusion = bf16[12,512,1024]{2,1,0:T(8,128)(2,1)S(1)} fusion(f32[12,512,1024]{2,1,0:T(8,128)} %get-tuple-element.101, f32[12,512]{1,0:T(8,128)S(1)} %get-tuple-element.100, f32[12,512,1024]{2,1,0:T(8,128)} %get-tuple-element.90, f32[12,512]{1,0:T(8,128)S(1)} %get-tuple-element.89), kind=kLoop, calls=%fused_computation.3 | loop fusion | flops 25165824 | bytes 62963712 | tf_op jit(solution)/shard_map/convert_element_type | solution.py:143
  498.3 17.4 %multiply_convert_fusion.1 = bf16[12,512,1024]{2,1,0:T(8,128)(2,1)S(1)} fusion(f32[12,512,1024]{2,1,0:T(8,128)} %get-tuple-element.99, f32[12,512]{1,0:T(8,128)S(1)} %get-tuple-element.98, f32[12,512,1024]{2,1,0:T(8,128)} %get-tuple-element.94, f32[12,512]{1,0:T(8,128)S(1)} %copy-done.73), kind=kLoop, calls=%fused_computation.5 | loop fusion | flops 25165824 | bytes 62963712 | tf_op jit(solution)/shard_map/convert_element_type | solution.py:143
  522.4 10.0 fusion.78
  535.8 10.1 convert_reduce_fusion.14
  545.9 10.2 convert_reduce_fusion.11
  556.2 6.0 fusion.108
  562.2 23.9 %reduce-scatter.11.cloned.1.call-done = bf16[512,1536]{0,1:T(8,128)(2,1)} async-done(((bf16[1024,1536]{0,1:T(8,128)(2,1)}), bf16[512,1536]{0,1:T(8,128)(2,1)}) %reduce-scatter.11.cloned.1.call-update) | async-done | bytes 1572880 | tf_op jit(solution)/shard_map/reduce_scatter | solution.py:163
  586.1 7.6 fusion.97
  604.6 22.5 %all-gather.16.cloned.1.call-done = bf16[1024,768]{1,0:T(8,128)(2,1)} async-done(((bf16[512,768]{1,0:T(8,128)(2,1)}), bf16[1024,768]{1,0:T(8,128)(2,1)}) %all-gather.16.cloned.1.call-update) | async-done | bytes 1572880 | tf_op jit(solution)/shard_map/all_gather | solution.py:88
  629.8 14.5 %fusion.203 = (f32[12,512]{1,0:T(8,128)S(1)}, f32[12,512,1024]{2,1,0:T(8,128)}) fusion(pred[512,1024]{1,0:T(8,128)(4,1)} %get-tuple-element.86, bf16[512,12,64]{0,2,1:T(8,128)(2,1)S(1)} %bitcast.318, bf16[1024,12,64]{0,2,1:T(8,128)(2,1)} %bitcast.312), kind=kOutput, calls=%fused_computation.315 | convolution fusion | flops 830473216 | bytes 28073984 | tf_op jit(solution)/shard_map/sub | solution.py:42
  644.3 11.6 all-gather.14.cloned.1.call-done
  658.4 10.9 fusion.113
  670.7 5.5 fusion.188
  676.3 7.1 convert_reduce_fusion.2
  694.6 16.8 %multiply_reduce_fusion.2 = (f32[12,512]{1,0:T(8,128)S(1)}, f32[12,512,1024]{2,1,0:T(8,128)}) fusion(f32[12,512,1024]{2,1,0:T(8,128)} %get-tuple-element.104, f32[12,512]{1,0:T(8,128)S(1)} %get-tuple-element.103, bf16[512,12,64]{0,2,1:T(8,128)(2,1)} %bitcast.341, bf16[1024,12,64]{0,2,1:T(8,128)(2,1)} %bitcast.327), kind=kOutput, calls=%fused_computation.8 | convolution fusion | flops 824174592 | bytes 52740096 | tf_op jit(solution)/shard_map/qhd,khd->hqk/dot_general | solution.py:139
  711.4 10.0 fusion.75
  721.5 16.3 %multiply_convert_fusion.2 = bf16[12,512,1024]{2,1,0:T(8,128)(2,1)S(1)} fusion(f32[12,512,1024]{2,1,0:T(8,128)} %get-tuple-element.109, f32[12,512]{1,0:T(8,128)S(1)} %get-tuple-element.108, f32[12,512,1024]{2,1,0:T(8,128)} %get-tuple-element.104, f32[12,512]{1,0:T(8,128)S(1)} %get-tuple-element.103), kind=kLoop, calls=%fused_computation.7 | loop fusion | flops 25165824 | bytes 62963712 | tf_op jit(solution)/shard_map/convert_element_type | solution.py:143
  750.6 6.3 fusion.133
  757.0 10.0 fusion.139
  767.0 13.7 %add_add_fusion = f32[3072,768]{1,0:T(8,128)} fusion(f32[3072,768]{1,0:T(8,128)} %fusion.139, f32[3072,768]{1,0:T(8,128)S(1)} %fusion.133, bf16[3,512,768]{2,1,0:T(8,128)(2,1)S(1)} %copy-done.7, f32[512,3072]{1,0:T(8,128)} %copy-done.18, f32[3072]{0:T(1024)S(1)} %copy-done.67), kind=kOutput, calls=%fused_computation.30 | convolution fusion | flops 2436366336 | bytes 35401728 | tf_op jit(solution)/shard_map/dot_general | solution.py:24
  790.1 7.6 add_add_fusion.1
  799.6 6.8 fusion.109
  806.4 8.7 convert_reduce_fusion.17
  819.4 5.2 add_add_fusion.2
  825.6 10.0 fusion.123
  835.7 9.1 fusion.124
  845.5 8.8 fusion.122
  864.3 40.5 %all-reduce.3 = (f32[8,768]{1,0:T(8,128)S(1)}, f32[3072]{0:T(1024)S(1)}) all-reduce(f32[8,768]{1,0:T(8,128)S(1)} %add_add_fusion.10, f32[3072]{0:T(1024)S(1)} %add_add_fusion.11), channel_id=9, replica_groups=mesh['dp'=16,'ctx'=2] {'dp','ctx'}, use_global_device_ids=true, to_apply=%region_64.65.clone | all-reduce | flops 9216 | bytes 73728
  913.1 121.3 %reduce-scatter.21.cloned.1.call-done = f32[96,768]{1,0:T(8,128)} async-done(((f32[3072,768]{1,0:T(8,128)}), f32[96,768]{1,0:T(8,128)}) %reduce-scatter.21.cloned.1.call-update) | async-done | bytes 294928 | tf_op jit(solution)/shard_map/reduce_scatter | solution.py:192
  1034.4 142.0 %reduce-scatter.19.cloned.1.call-done = f32[24,3072]{1,0:T(8,128)} async-done(((f32[768,3072]{1,0:T(8,128)}), f32[24,3072]{1,0:T(8,128)}) %reduce-scatter.19.cloned.1.call-update) | async-done | bytes 294928 | tf_op jit(solution)/shard_map/reduce_scatter | solution.py:191
  1176.3 124.5 %reduce-scatter.15.cloned.1.call-done = f32[24,2304]{1,0:T(8,128)} async-done(((f32[768,2304]{1,0:T(8,128)}), f32[24,2304]{1,0:T(8,128)}) %reduce-scatter.15.cloned.1.call-update) | async-done | bytes 221200 | tf_op jit(solution)/shard_map/reduce_scatter | solution.py:189
  (471 shorter events, 160.4 us)
Async XLA Ops:
  7.2 75.1 %copy-start.3 = (bf16[3,512,768]{2,1,0:T(8,128)(2,1)S(1)}, bf16[3,512,768]{2,1,0:T(8,128)(2,1)}, u32[]{:S(2)}) copy-start(bf16[3,512,768]{2,1,0:T(8,128)(2,1)} %param.9) | copy-start | bytes 7077892
  7.2 75.7 %all-gather.12.cloned.1.call-start = ((), (), s32[]{:S(2)}) async-start(), calls=%async_computation.7 | async-start | bytes 3649536 | tf_op jit(solution)/shard_map/all_gather | solution.py:69
  7.9 139.4 %all-gather.26.cloned.1.call-start = ((), (), s32[]{:S(2)}) async-start(), calls=%async_computation.14 | async-start | bytes 2359296 | tf_op jit(solution)/shard_map/all_gather | solution.py:88
  79.6 10.7 copy-start.61
  79.6 10.7 copy-start.104
  79.6 15.2 %copy-start.68 = (f32[768]{0:T(1024)}, f32[768]{0:T(1024)S(1)}, u32[]{:S(2)}) copy-start(f32[768]{0:T(1024)S(1)} %get-tuple-element.44) | copy-start | bytes 9220
  79.6 15.2 %copy-start.70 = (f32[768]{0:T(1024)}, f32[768]{0:T(1024)S(1)}, u32[]{:S(2)}) copy-start(f32[768]{0:T(1024)S(1)} %get-tuple-element.45) | copy-start | bytes 9220
  79.6 208.7 %copy-start.124 = (f32[768]{0:T(1024)}, f32[768]{0:T(1024)S(1)}, u32[]{:S(2)}) copy-start(f32[768]{0:T(1024)S(1)} %get-tuple-element.43) | copy-start | bytes 9220
  79.6 322.4 %copy-start.107 = (f32[768]{0:T(1024)}, f32[768]{0:T(1024)S(1)}, u32[]{:S(2)}) copy-start(f32[768]{0:T(1024)S(1)} %get-tuple-element.42) | copy-start | bytes 9220
  79.6 336.2 %copy-start.64 = (f32[768]{0:T(1024)}, f32[768]{0:T(1024)S(1)}, u32[]{:S(2)}) copy-start(f32[768]{0:T(1024)S(1)} %get-tuple-element.40) | copy-start | bytes 9220
  90.2 74.2 %all-gather.24.cloned.1.call-start = ((), (), s32[]{:S(2)}) async-start(), calls=%async_computation.13 | async-start | bytes 2359296 | tf_op jit(solution)/shard_map/all_gather | solution.py:89
  97.9 75.0 %all-gather.30.cloned.1.call-start = ((), (), s32[]{:S(2)}) async-start(), calls=%async_computation.16 | async-start | bytes 2359296 | tf_op jit(solution)/shard_map/all_gather | solution.py:88
  100.4 101.2 %all-gather.28.cloned.1.call-start = ((), (), s32[]{:S(2)}) async-start(), calls=%async_computation.15 | async-start | bytes 2359296 | tf_op jit(solution)/shard_map/all_gather | solution.py:89
  101.0 157.5 %all-gather.18.cloned.1.call-start = ((), (), s32[]{:S(2)}) async-start(), calls=%async_computation.10 | async-start | bytes 1216512 | tf_op jit(solution)/shard_map/all_gather | solution.py:70
  101.5 222.5 %all-gather.20.cloned.1.call-start = ((), (), s32[]{:S(2)}) async-start(), calls=%async_computation.11 | async-start | bytes 4866048 | tf_op jit(solution)/shard_map/all_gather | solution.py:71
  102.3 287.1 %all-gather.22.cloned.1.call-start = ((), (), s32[]{:S(2)}) async-start(), calls=%async_computation.12 | async-start | bytes 4866048 | tf_op jit(solution)/shard_map/all_gather | solution.py:72
  103.0 453.1 %reduce-scatter.13.cloned.1.call-start = ((), (), s32[]{:S(2)}) async-start(), calls=%async_computation.19 | async-start | bytes 4718592 | tf_op jit(solution)/shard_map/reduce_scatter | solution.py:163
  141.0 263.9 %copy-start.66 = (f32[3072]{0:T(1024)}, f32[3072]{0:T(1024)S(1)}, u32[]{:S(2)}) copy-start(f32[3072]{0:T(1024)S(1)} %convert_element_type.267) | copy-start | bytes 36868
  164.4 39.7 %copy-start.72 = (f32[12,512]{1,0:T(8,128)}, f32[12,512]{1,0:T(8,128)S(1)}, u32[]{:S(2)}) copy-start(f32[12,512]{1,0:T(8,128)S(1)} %get-tuple-element.93) | copy-start | bytes 73732
  261.0 154.8 %copy-start.81 = (f32[512]{0:T(512)}, f32[512]{0:T(512)S(1)}, u32[]{:S(2)}) copy-start(f32[512]{0:T(512)S(1)} %broadcast_multiply_fusion.2) | copy-start | bytes 6148
  277.4 10.9 copy-start.139
  289.3 126.6 %copy-start.74 = (f32[512]{0:T(512)}, f32[512]{0:T(512)S(1)}, u32[]{:S(2)}) copy-start(f32[512]{0:T(512)S(1)} %broadcast_multiply_fusion) | copy-start | bytes 6148
  290.7 125.1 %copy-start.116 = (f32[512]{0:T(512)}, f32[512]{0:T(512)S(1)}, u32[]{:S(2)}) copy-start(f32[512]{0:T(512)S(1)} %fusion.154) | copy-start | bytes 6148
  290.7 125.1 %copy-start.83 = (f32[512]{0:T(512)}, f32[512]{0:T(512)S(1)}, u32[]{:S(2)}) copy-start(f32[512]{0:T(512)S(1)} %fusion.156) | copy-start | bytes 6148
  324.0 65.4 %copy-start.6 = (bf16[3,512,768]{2,1,0:T(8,128)(2,1)S(1)}, bf16[3,512,768]{2,1,0:T(8,128)(2,1)}, u32[]{:S(2)}) copy-start(bf16[3,512,768]{2,1,0:T(8,128)(2,1)} %param.17) | copy-start | bytes 7077892
  418.9 34.2 %copy-start.46 = (bf16[512,768]{1,0:T(8,128)(2,1)}, bf16[512,768]{1,0:T(8,128)(2,1)S(1)}, u32[]{:S(2)}) copy-start(bf16[512,768]{1,0:T(8,128)(2,1)S(1)} %get-tuple-element.75) | copy-start | bytes 2359300
  442.0 11.1 copy-start.141
  475.1 16.4 %copy-start.32 = (bf16[512,768]{0,1:T(8,128)(2,1)S(1)}, bf16[512,768]{0,1:T(8,128)(2,1)}, u32[]{:S(2)}) copy-start(bf16[512,768]{0,1:T(8,128)(2,1)} %copy.76) | copy-start | bytes 2359300
  498.2 87.9 %reduce-scatter.11.cloned.1.call-start = ((), (), s32[]{:S(2)}) async-start(), calls=%async_computation.18 | async-start | bytes 4718592 | tf_op jit(solution)/shard_map/reduce_scatter | solution.py:163
  498.2 21.9 %copy-start.30 = (bf16[512,768]{0,1:T(8,128)(2,1)S(1)}, bf16[512,768]{0,1:T(8,128)(2,1)}, u32[]{:S(2)}) copy-start(bf16[512,768]{0,1:T(8,128)(2,1)} %copy-done.29) | copy-start | bytes 2359300
  534.4 92.8 %all-gather.16.cloned.1.call-start = ((), (), s32[]{:S(2)}) async-start(), calls=%async_computation.9 | async-start | bytes 2359296 | tf_op jit(solution)/shard_map/all_gather | solution.py:88
  535.8 58.0 %copy-start.100 = (f32[512]{0:T(512)}, f32[512]{0:T(512)S(1)}, u32[]{:S(2)}) copy-start(f32[512]{0:T(512)S(1)} %broadcast_multiply_fusion.5) | copy-start | bytes 6148
  556.1 29.9 %copy-start.4 = (bf16[3,512,768]{2,1,0:T(8,128)(2,1)S(1)}, bf16[3,512,768]{2,1,0:T(8,128)(2,1)}, u32[]{:S(2)}) copy-start(bf16[3,512,768]{2,1,0:T(8,128)(2,1)} %param.9) | copy-start | bytes 7077892
  556.1 29.9 %copy-start.62 = (f32[768]{0:T(1024)S(1)}, f32[768]{0:T(1024)}, u32[]{:S(2)}) copy-start(f32[768]{0:T(1024)} %copy-done.61) | copy-start | bytes 9220
  556.1 29.9 %copy-start.79 = (f32[512]{0:T(512)S(1)}, f32[512]{0:T(512)}, u32[]{:S(2)}) copy-start(f32[512]{0:T(512)} %copy-done.78) | copy-start | bytes 6148
  556.1 29.9 %copy-start.96 = (f32[512]{0:T(512)S(1)}, f32[512]{0:T(512)}, u32[]{:S(2)}) copy-start(f32[512]{0:T(512)} %copy-done.95) | copy-start | bytes 6148
  599.8 56.0 %all-gather.14.cloned.1.call-start = ((), (), s32[]{:S(2)}) async-start(), calls=%async_computation.8 | async-start | bytes 2359296 | tf_op jit(solution)/shard_map/all_gather | solution.py:89
  604.6 210.6 %reduce-scatter.9.cloned.1.call-start = ((), (), s32[]{:S(2)}) async-start(), calls=%async_computation.17 | async-start | bytes 4718592 | tf_op jit(solution)/shard_map/reduce_scatter | solution.py:163
  658.4 10.9 copy-start.125
  658.4 10.9 copy-start.142
  670.3 16.7 %copy-start.22 = (f32[512,768]{1,0:T(8,128)}, f32[512,768]{1,0:T(8,128)S(1)}, u32[]{:S(2)}) copy-start(f32[512,768]{1,0:T(8,128)S(1)} %get-tuple-element.106) | copy-start | bytes 4718596
  670.7 12.7 slice-start.2
  744.3 168.8 %reduce-scatter.17.cloned.1.call-start = ((), (), s32[]{:S(2)}) async-start(), calls=%async_computation.21 | async-start | bytes 2433024 | tf_op jit(solution)/shard_map/reduce_scatter | solution.py:190
  750.6 283.8 %reduce-scatter.21.cloned.1.call-start = ((), (), s32[]{:S(2)}) async-start(), calls=%async_computation.23 | async-start | bytes 9732096 | tf_op jit(solution)/shard_map/reduce_scatter | solution.py:192
  780.7 395.6 %reduce-scatter.19.cloned.1.call-start = ((), (), s32[]{:S(2)}) async-start(), calls=%async_computation.22 | async-start | bytes 9732096 | tf_op jit(solution)/shard_map/reduce_scatter | solution.py:191
  797.8 503.1 %reduce-scatter.15.cloned.1.call-start = ((), (), s32[]{:S(2)}) async-start(), calls=%async_computation.20 | async-start | bytes 7299072 | tf_op jit(solution)/shard_map/reduce_scatter | solution.py:189
  861.1 44.9 %copy-start.92 = (f32[512]{0:T(512)S(1)}, f32[512]{0:T(512)}, u32[]{:S(2)}) copy-start(f32[512]{0:T(512)} %copy-done.91) | copy-start | bytes 6148
  861.2 44.9 %copy-start.99 = (f32[512]{0:T(512)S(1)}, f32[512]{0:T(512)}, u32[]{:S(2)}) copy-start(f32[512]{0:T(512)} %copy-done.98) | copy-start | bytes 6148
  (121 other events, 522.2 us)
Sparse Core Ops, SparseCore 0:
  10.9 63.1 all-gather.11
  90.4 23.5 all-gather.25
  116.1 28.0 all-gather.23
  145.6 27.1 all-gather.29
  174.3 27.2 all-gather.27
  204.3 54.1 all-gather.17
  261.4 62.5 all-gather.19
  326.9 62.4 all-gather.21
  498.3 42.1 reduce-scatter.12
  542.7 43.3 reduce-scatter.10
  599.9 27.1 all-gather.15
  628.6 27.1 all-gather.13
  744.4 43.3 reduce-scatter.8
  794.3 98.9 reduce-scatter.16
  899.7 134.6 reduce-scatter.20
  1041.7 134.5 reduce-scatter.18
  1182.4 118.3 reduce-scatter.14
where the time goes:
time: 1310 us
  waiting for transfers between devices  614 us (47%)
  matrix products  382 us (29%)
  blocking collectives  149 us (11%)
  other arithmetic  83.9 us (6%)
  local copies, waits for them, and re-layouts  60.7 us (5%)
  between operations  16.4 us (1%)
    reduce_scatter x1, waiting for transfers between devices, on_device(): lax.psum_scatter(grad_up, ('dp', 'ctx'), scatter_dimension=0, tiled=True)  142 us
    reduce_scatter x1, waiting for transfers between devices, on_device(): lax.psum_scatter(grad_qkv, ('dp', 'ctx'), scatter_dimension=0, tiled=True)  125 us
    reduce_scatter x1, waiting for transfers between devices, on_device(): lax.psum_scatter(grad_down, ('dp', 'ctx'), scatter_dimension=0, tiled=True)  121 us
    unnamed x2, blocking collectives  78 us
    all_gather x1, blocking collectives, on_device(): lax.all_gather(shards[4], ('dp', 'ctx'), axis=1, tiled=True)  70.7 us
    dot_general x12, matrix products, contract_rows(): lax.dot_general(left, right, (((0,), (0,)), ((), ())), preferred_element_...  66.7 us
    all_gather x1, waiting for transfers between devices, on_device(): lax.all_gather(shards[3], ('dp', 'ctx'), axis=0, tiled=True)  57.1 us
    dot_general x12, matrix products, contract_cols(): lax.dot_general(left, right, (((1,), (1,)), ((), ())), preferred_element_...  56.4 us
  transfers between devices with their start and end apart: 17, of which 11 were waited for; matrix products, arithmetic and copies ran while one was open for 23% of the time, Pallas kernels for 0%

commit v1 on v0

v1 whole, which is shorter than its diff:
```python
import functools

import jax
import jax.numpy as jnp
from jax import lax
from jax.experimental import pallas as pl
from jax.experimental.pallas import tpu as pltpu
from jax.sharding import PartitionSpec as P

HEADS = 12
EPSILON = 1e-05
LANES = 128
BLOCK = 256
MASKED = -1e30
F32 = jnp.float32
BF16 = jnp.bfloat16


def layer_norm(values, norm_gain, norm_shift):
    average = jnp.mean(values, -1, keepdims=True)
    centred = values - average
    variance = jnp.mean(centred * centred, -1, keepdims=True)
    return centred * lax.rsqrt(variance + EPSILON) * norm_gain + norm_shift


def gelu_tanh(pre_act):
    return jax.nn.gelu(pre_act, approximate=True)


def dot(left, right):
    return jnp.dot(left, right, preferred_element_type=F32)


def contract_rows(left, right):
    return lax.dot_general(left, right, (((0,), (0,)), ((), ())), preferred_element_type=F32)


def contract_cols(left, right):
    return lax.dot_general(left, right, (((1,), (1,)), ((), ())), preferred_element_type=F32)


def split_pair(pair, left_lanes):
    zero = jnp.zeros_like(pair)
    return jnp.where(left_lanes, pair, zero), jnp.where(left_lanes, zero, pair)


def fill_bias(place_ref, q_seg_ref, k_seg_ref, bias_ref):
    rows = q_seg_ref.shape[0]
    for block in range(bias_ref.shape[0]):
        row = lax.broadcasted_iota(jnp.int32, (rows, BLOCK), 0) + place_ref[0]
        col = lax.broadcasted_iota(jnp.int32, (rows, BLOCK), 1) + block * BLOCK
        same = q_seg_ref[...] == k_seg_ref[:, block * BLOCK : (block + 1) * BLOCK]
        bias_ref[block] = jnp.where((col <= row) & same, 0.0, MASKED)


def attend_kernel(
    factor, first_ref, place_ref, q_ref, k_ref, v_ref, q_seg_ref, k_seg_ref, o_ref, lse_ref, bias_ref
):
    @pl.when(pl.program_id(0) == 0)
    def _():
        fill_bias(place_ref, q_seg_ref, k_seg_ref, bias_ref)

    left_lanes = lax.broadcasted_iota(jnp.int32, (BLOCK, LANES), 1) < LANES // 2
    for q_block in range(q_ref.shape[0] // BLOCK):
        span = slice(q_block * BLOCK, (q_block + 1) * BLOCK)
        queries = split_pair((q_ref[span, :] * factor).astype(BF16), left_lanes)

        def step(block, carry):
            place = pl.ds(pl.multiple_of(block * BLOCK, BLOCK), BLOCK)
            keys, values = k_ref[place, :], v_ref[place, :]
            bias = bias_ref[block, span, :]
            after = []
            for query, (top, total, summed) in zip(queries, carry):
                scores = contract_cols(query, keys) + bias
                new_top = jnp.maximum(top, jnp.max(scores, -1, keepdims=True))
                expo = jnp.exp(scores - new_top)
                shrink = jnp.exp(top - new_top)
                total = total * shrink + jnp.sum(expo, -1, keepdims=True)
                summed = summed * shrink + dot(expo.astype(BF16), values)
                after.append((new_top, total, summed))
            return tuple(after)

        begin = (
            jnp.full((BLOCK, 1), MASKED, F32),
            jnp.zeros((BLOCK, 1), F32),
            jnp.zeros((BLOCK, LANES), F32),
        )
        last = place_ref[0] // BLOCK + q_block + 1
        (top_a, total_a, sum_a), (top_b, total_b, sum_b) = lax.fori_loop(
            first_ref[q_block], last, step, (begin, begin)
        )
        o_ref[span, :] = jnp.where(left_lanes, sum_a / total_a, sum_b / total_b).astype(BF16)
        lse_ref[span, :] = jnp.where(
            left_lanes, top_a + jnp.log(total_a), top_b + jnp.log(total_b)
        )


def attend_back_kernel(
    factor,
    first_ref,
    place_ref,
    q_ref,
    k_ref,
    v_ref,
    q_seg_ref,
    k_seg_ref,
    o_ref,
    lse_ref,
    do_ref,
    dq_ref,
    dk_ref,
    dv_ref,
    bias_ref,
    dk_sum,
    dv_sum,
):
    @pl.when(pl.program_id(0) == 0)
    def _():
        fill_bias(place_ref, q_seg_ref, k_seg_ref, bias_ref)

    dk_sum[...] = jnp.zeros_like(dk_sum)
    dv_sum[...] = jnp.zeros_like(dv_sum)
    left_lanes = lax.broadcasted_iota(jnp.int32, (BLOCK, LANES), 1) < LANES // 2
    for q_block in range(q_ref.shape[0] // BLOCK):
        span = slice(q_block * BLOCK, (q_block + 1) * BLOCK)
        queries = split_pair((q_ref[span, :] * factor).astype(BF16), left_lanes)
        grads = split_pair(do_ref[span, :], left_lanes)
        products = do_ref[span, :].astype(F32) * o_ref[span, :].astype(F32)
        deltas = [jnp.sum(part, -1, keepdims=True) for part in split_pair(products, left_lanes)]
        tops = (lse_ref[span, 0:1], lse_ref[span, LANES // 2 : LANES // 2 + 1])

        def step(block, grad_query):
            place = pl.ds(pl.multiple_of(block * BLOCK, BLOCK), BLOCK)
            keys, values = k_ref[place, :], v_ref[place, :]
            bias = bias_ref[block, span, :]
            grad_key = dk_sum[place, :]
            grad_value = dv_sum[place, :]
            for query, grad, delta, top, key_half in zip(
                queries, grads, deltas, tops, split_pair(keys, left_lanes)
            ):
                probs = jnp.exp(contract_cols(query, keys) + bias - top)
                grad_score = (probs * (contract_cols(grad, values) - delta)).astype(BF16)
                grad_value = grad_value + contract_rows(probs.astype(BF16), grad)
                grad_key = grad_key + contract_rows(grad_score, query)
                grad_query = grad_query + dot(grad_score, key_half)
            dk_sum[place, :] = grad_key
            dv_sum[place, :] = grad_value
            return grad_query

        last = place_ref[0] // BLOCK + q_block + 1
        grad_query = lax.fori_loop(
            first_ref[q_block], last, step, jnp.zeros((BLOCK, LANES), F32)
        )
        dq_ref[span, :] = (grad_query * factor).astype(BF16)
    dk_ref[...] = dk_sum[...].astype(BF16)
    dv_ref[...] = dv_sum[...].astype(BF16)


def attention_call(kernel, name, first, place, operands, out_types, sums, products):
    query, keys = operands[0], operands[1]
    rows, model_width = query.shape
    length = keys.shape[0]

    def spec(array):
        if array.shape[1] == model_width:
            return pl.BlockSpec((array.shape[0], LANES), lambda pair, *_: (0, pair))
        return pl.BlockSpec(array.shape, lambda pair, *_: (0, 0))

    scratch = [pltpu.VMEM((length // BLOCK, rows, BLOCK), F32)]
    scratch += [pltpu.VMEM((length, LANES), F32)] * sums
    return pl.pallas_call(
        kernel,
        grid_spec=pltpu.PrefetchScalarGridSpec(
            num_scalar_prefetch=2,
            grid=(model_width // LANES,),
            in_specs=[spec(array) for array in operands],
            out_specs=[spec(array) for array in out_types],
            scratch_shapes=scratch,
        ),
        out_shape=out_types,
        name=name,
        compiler_params=pltpu.CompilerParams(vmem_limit_bytes=40 * 1024 * 1024),
        cost_estimate=pl.CostEstimate(
            flops=products * 8 * rows * length * model_width,
            bytes_accessed=16 * length * model_width,
            transcendentals=HEADS * rows * length,
        ),
    )(first, place, *operands)


def on_device(
    tokens, segments, qkv_weight, out_weight, up_weight, down_weight, vectors, up_bias, cotangent
):
    micro_count, span_rows, width = tokens.shape
    head_dim = width // HEADS
    factor = head_dim ** (-0.5)
    row_share = qkv_weight.shape[0]
    both = ("dp", "ctx")
    ctx_size = lax.axis_size("ctx")
    ctx_place = lax.axis_index("ctx")
    q_start = ctx_place * span_rows
    neighbours = ctx_size == 2

    def gather(shard):
        return lax.all_gather(shard, both, axis=0, tiled=True)

    def scatter(whole):
        return lax.psum_scatter(whole.astype(BF16), both, scatter_dimension=0, tiled=True)

    vec_count = vectors.shape[0]
    bias_count = up_bias.shape[0] // row_share
    extra_count = vec_count + bias_count
    extra = jnp.concatenate([vectors.T, up_bias.reshape(row_share, bias_count)], 1)
    extra = jnp.pad(extra, ((0, 0), (0, LANES - extra_count)))
    wide = gather(jnp.concatenate([qkv_weight, extra], 1))
    w_out = gather(out_weight)
    w_up = gather(up_weight)
    w_down = gather(down_weight)
    w_qkv = wide[:, : 3 * width]
    small = wide[:, 3 * width : 3 * width + extra_count].astype(F32)
    vec_rows = small[:, :vec_count].T
    bias_all = small[:, vec_count:].reshape(-1)

    token_rows = tokens.reshape(micro_count * span_rows, width).astype(F32)
    hidden = layer_norm(token_rows, vec_rows[0], vec_rows[1]).astype(BF16)
    mixed_kv = dot(hidden, w_qkv[:, width:])
    key_value = jnp.concatenate(
        [mixed_kv[:, :width].astype(BF16), (mixed_kv[:, width:] + vec_rows[3]).astype(BF16)], 1
    ).reshape(micro_count, span_rows, 2 * width)
    query_all = (dot(hidden, w_qkv[:, :width]) + vec_rows[2]).astype(BF16)
    query_all = query_all.reshape(micro_count, span_rows, width)

    saved = []
    attended = []
    for micro in range(micro_count):
        own_kv = key_value[micro]
        seq_segs = segments[micro]
        own_segs = lax.dynamic_slice_in_dim(seq_segs, q_start, span_rows)
        if neighbours:
            before = lax.ppermute(own_kv, "ctx", [(0, 1)])
            all_kv = jnp.concatenate([before, own_kv], 0)
            k_segs = jnp.concatenate(
                [jnp.where(ctx_place == 0, -1, seq_segs[:span_rows]), own_segs], 0
            )
            place = jnp.full((1,), span_rows, jnp.int32)
        else:
            all_kv = lax.all_gather(own_kv, "ctx", axis=0, tiled=True)
            k_segs = seq_segs
            place = jnp.full((1,), q_start, jnp.int32)
        starts = own_segs[::BLOCK]
        first = jnp.sum((k_segs[None, :] < starts[:, None]).astype(jnp.int32), 1) // BLOCK
        operands = (
            query_all[micro],
            all_kv[:, :width],
            all_kv[:, width:],
            own_segs[:, None],
            k_segs[None, :],
        )
        low_rows = jax.ShapeDtypeStruct((span_rows, width), BF16)
        out, lse = attention_call(
            functools.partial(attend_kernel, factor),
            "attend",
            first,
            place,
            operands,
            [low_rows, jax.ShapeDtypeStruct((span_rows, width), F32)],
            0,
            1,
        )
        saved.append((first, place, operands, out, lse))
        attended.append(out)
    attended = jnp.concatenate(attended, 0)

    middle = token_rows + dot(attended, w_out) + vec_rows[4]
    inner = layer_norm(middle, vec_rows[5], vec_rows[6]).astype(BF16)
    pre_act = dot(inner, w_up) + bias_all
    active = gelu_tanh(pre_act).astype(BF16)
    result = (middle + dot(active, w_down) + vec_rows[7]).astype(BF16)

    grad_low = cotangent.reshape(micro_count * span_rows, width)
    grad_rows = grad_low.astype(F32)
    own_down = scatter(contract_rows(active, grad_low))
    grad_bdown = jnp.sum(grad_rows, 0)
    grad_act = contract_cols(grad_low, w_down)
    grad_pre = jax.vjp(gelu_tanh, pre_act)[1](grad_act)[0].astype(BF16)
    own_up = scatter(contract_rows(inner, grad_pre))
    grad_bias = jnp.sum(grad_pre.astype(F32), 0)
    grad_inner = contract_cols(grad_pre, w_up)
    norm_two_back = jax.vjp(layer_norm, middle, vec_rows[5], vec_rows[6])[1]
    grad_mid_norm, grad_gain_two, grad_shift_two = norm_two_back(grad_inner)
    grad_middle = grad_rows + grad_mid_norm
    grad_branch = grad_middle.astype(BF16)
    own_out = scatter(contract_rows(attended, grad_branch))
    grad_bout = jnp.sum(grad_branch.astype(F32), 0)
    grad_att = contract_cols(grad_branch, w_out).astype(BF16)
    grad_att = grad_att.reshape(micro_count, span_rows, width)

    grad_queries = []
    grad_kvs = []
    for micro in range(micro_count):
        first, place, operands, out, lse = saved[micro]
        low_keys = jax.ShapeDtypeStruct(operands[1].shape, BF16)
        grad_query, grad_key, grad_value = attention_call(
            functools.partial(attend_back_kernel, factor),
            "attend_back",
            first,
            place,
            operands + (out, lse, grad_att[micro]),
            [jax.ShapeDtypeStruct((span_rows, width), BF16), low_keys, low_keys],
            2,
            3,
        )
        grad_queries.append(grad_query)
        kv_terms = jnp.concatenate([grad_key, grad_value], 1)
        if neighbours:
            theirs = lax.ppermute(kv_terms[:span_rows], "ctx", [(1, 0)])
            own = kv_terms[span_rows:].astype(F32) + theirs.astype(F32)
        else:
            own = lax.psum_scatter(kv_terms, "ctx", scatter_dimension=0, tiled=True)
        grad_kvs.append(own.astype(BF16))
    grad_query = jnp.concatenate(grad_queries, 0)
    grad_kv = jnp.concatenate(grad_kvs, 0)
    grad_mixed = jnp.concatenate([grad_query, grad_kv], 1)
    grad_qkv = contract_rows(hidden, grad_mixed)
    column_sums = jnp.sum(grad_mixed.astype(F32), 0)
    grad_hidden = contract_cols(grad_mixed, w_qkv)
    norm_one_back = jax.vjp(layer_norm, token_rows, vec_rows[0], vec_rows[1])[1]
    grad_tok_norm, grad_gain_one, grad_shift_one = norm_one_back(grad_hidden)
    input_grad = grad_middle + grad_tok_norm
    grad_vec = jnp.stack(
        [
            grad_gain_one,
            grad_shift_one,
            column_sums[:width],
            column_sums[2 * width :],
            grad_bout,
            grad_gain_two,
            grad_shift_two,
            grad_bdown,
        ]
    )
    grad_extra = jnp.concatenate([grad_vec.T, grad_bias.reshape(width, bias_count)], 1)
    grad_extra = jnp.pad(grad_extra, ((0, 0), (0, LANES - extra_count)))
    own_wide = scatter(jnp.concatenate([grad_qkv, grad_extra], 1)).astype(F32)
    own_small = own_wide[:, 3 * width : 3 * width + extra_count]
    return (
        result.reshape(tokens.shape),
        input_grad.reshape(tokens.shape),
        own_wide[:, : 3 * width],
        own_out.astype(F32),
        own_up.astype(F32),
        own_down.astype(F32),
        own_small[:, :vec_count].T,
        own_small[:, vec_count:].reshape(-1),
    )


def solution(mesh):
    rows = P(("dp", "ctx"), None)
    spans = P("dp", "ctx", None)
    tail = (rows, rows, rows, rows, P(None, ("dp", "ctx")), P(("dp", "ctx")))
    return jax.shard_map(
        on_device,
        mesh=mesh,
        in_specs=(spans, P("dp", None)) + tail + (spans,),
        out_specs=(spans, spans) + tail,
        check_vma=False,
    )
```

time: 1310 us -> 776 us (0.59)
  matrix products: 382 us -> 133 us
  waiting for transfers between devices: 614 us -> 374 us
  blocking collectives: 149 us -> 0 us
  Pallas kernels: 0 us -> 118 us
  local copies, waits for them, and re-layouts: 60.7 us -> 37.2 us
    reduce_scatter x7 -> x3, waiting for transfers between devices: 412 us -> 107 us  [scatter(): lax.psum_scatter(whole.astype(BF16), both, scatter_dimension=0, tiled=True)]
    dot_general x27 -> x5, matrix products: 215 us -> 48 us  [dot(): return jnp.dot(left, right, preferred_element_type=F32)]
    all_gather x10 -> x4, waiting for transfers between devices: 199 us -> 71.6 us  [gather(): return lax.all_gather(shard, both, axis=0, tiled=True)]
    pallas_call x0 -> x6, Pallas kernels: none -> 118 us  [attention_call(): pl.pallas_call(kernel, grid_spec=pltpu.PrefetchScalarGridSpec(num_scalar_...]
    unnamed x17 -> x9, waiting for transfers between devices: 3.33 us -> 103 us
    ppermute x0 -> x6, waiting for transfers between devices: none -> 91.4 us  [the longest x3 60 us: on_device(): before = lax.ppermute(own_kv, 'ctx', [(0, 1)])]
    unnamed x2 -> x0, blocking collectives: 78 us -> none
    all_gather x1 -> x0, blocking collectives: 70.7 us -> none  [on_device(): lax.all_gather(shards[4], ('dp', 'ctx'), axis=1, tiled=True)]
  transfers between devices with their start and end apart: 17 -> 14, of which waited for: 11 -> 9; matrix products, arithmetic and copies ran while one was open for 23% -> 23% of each run, Pallas kernels for 0% -> 15%
where the time goes in v1:
time: 776 us; the launch traced here: 769 us
  waiting for transfers between devices  374 us (48%)
  matrix products  133 us (17%)
  Pallas kernels  118 us (15%)
  other arithmetic  77.3 us (10%)
  local copies, waits for them, and re-layouts  37.2 us (5%)
  between operations  15.7 us (2%)
  starting transfers between devices  14.7 us (2%)
    pallas_call x6, Pallas kernels, attention_call(): pl.pallas_call(kernel, grid_spec=pltpu.PrefetchScalarGridSpec(num_scalar_...  118 us
    reduce_scatter x3, waiting for transfers between devices, scatter(): lax.psum_scatter(whole.astype(BF16), both, scatter_dimension=0, tiled=True)  107 us
    unnamed x9, waiting for transfers between devices  103 us
    all_gather x4, waiting for transfers between devices, gather(): return lax.all_gather(shard, both, axis=0, tiled=True)  71.6 us
    ppermute x3, waiting for transfers between devices, on_device(): before = lax.ppermute(own_kv, 'ctx', [(0, 1)])  60 us
    dot_general x5, matrix products, dot(): return jnp.dot(left, right, preferred_element_type=F32)  48 us
    dot_general x4, matrix products, contract_cols(): lax.dot_general(left, right, (((1,), (1,)), ((), ())), preferred_element_...  46.9 us
    dot_general x4, matrix products, contract_rows(): lax.dot_general(left, right, (((0,), (0,)), ((), ())), preferred_element_...  37.6 us
  transfers between devices with their start and end apart: 14, of which 9 were waited for; matrix products, arithmetic and copies ran while one was open for 23% of the time, Pallas kernels for 15%

profile of v1, /device:TPU:0, one launch (start us, length us, event | category | flops | bytes accessed | tf_op | source)
XLA Modules:
  0.0 769.4 jit_solution(11529635228642335489)
XLA Ops:
  12.7 2.0 convert_reduce_fusion
  16.8 58.2 %all-gather.5.cloned.1.call-done = bf16[768,2432]{1,0:T(8,128)(2,1)} async-done(((bf16[24,2432]{1,0:T(8,128)(2,1)}), bf16[768,2432]{1,0:T(8,128)(2,1)}) %all-gather.5.cloned.1.call-update) | async-done | bytes 3735568 | tf_op jit(solution)/shard_map/all_gather | solution.py:205
  76.9 1.6 slice_reduce_fusion
  81.4 3.8 fusion.23
  86.3 2.4 pad_maximum_fusion.2
  88.6 4.5 collective-permute-start
  93.8 2.4 collective-permute-start.1
  97.4 2.5 collective-permute-start.2
  99.9 5.5 add_convert_fusion.2
  105.7 1.8 fusion.48
  107.5 22.7 %collective-permute-done = bf16[512,1536]{1,0:T(8,128)(2,1)} collective-permute-done((bf16[512,1536]{1,0:T(8,128)(2,1)}, bf16[512,1536]{1,0:T(8,128)(2,1)}, u32[]{:S(2)}, u32[]{:S(2)}) %collective-permute-start) | collective-permute-done | bytes 1572896 | tf_op jit(solution)/shard_map/ppermute | solution.py:240
  130.2 2.1 pad_maximum_fusion.4
  132.3 18.7 %attend.3 = (bf16[512,768]{1,0:T(8,128)(2,1)S(1)}, f32[512,768]{1,0:T(8,128)S(1)}) custom-call(s32[2]{0:T(128)S(1)} %and_select_fusion.2.first_ref, s32[1]{0:T(128)} %constant.65.clone.1.place_ref, bf16[512,768]{1,0:T(8,128)(2,1)S(1)} %get-tuple-element.105.q_ref, bf16[1024,768]{1,0:T(8,128)(2,1)S(1)} %get-tuple-element.99.k_ref, ...), custom_call_target="tpu_custom_call" | custom-call | flops 3221225472 | bytes 12582912 | tf_op jit(solution)/shard_map/attend/pallas_call | solution.py:171
  152.0 17.1 %collective-permute-done.1 = bf16[512,1536]{1,0:T(8,128)(2,1)} collective-permute-done((bf16[512,1536]{1,0:T(8,128)(2,1)}, bf16[512,1536]{1,0:T(8,128)(2,1)}, u32[]{:S(2)}, u32[]{:S(2)}) %collective-permute-start.1) | collective-permute-done | bytes 1572896 | tf_op jit(solution)/shard_map/ppermute | solution.py:240
  170.8 18.5 %attend.4 = (bf16[512,768]{1,0:T(8,128)(2,1)S(1)}, f32[512,768]{1,0:T(8,128)S(1)}) custom-call(s32[2]{0:T(128)S(1)} %and_select_fusion.1.first_ref, s32[1]{0:T(128)} %constant.65.clone.1.place_ref, bf16[512,768]{1,0:T(8,128)(2,1)S(1)} %get-tuple-element.104.q_ref, bf16[1024,768]{1,0:T(8,128)(2,1)S(1)} %get-tuple-element.97.k_ref, ...), custom_call_target="tpu_custom_call" | custom-call | flops 3221225472 | bytes 12582912 | tf_op jit(solution)/shard_map/attend/pallas_call | solution.py:171
  190.3 20.3 %collective-permute-done.2 = bf16[512,1536]{1,0:T(8,128)(2,1)} collective-permute-done((bf16[512,1536]{1,0:T(8,128)(2,1)}, bf16[512,1536]{1,0:T(8,128)(2,1)}, u32[]{:S(2)}, u32[]{:S(2)}) %collective-permute-start.2) | collective-permute-done | bytes 1572896 | tf_op jit(solution)/shard_map/ppermute | solution.py:240
  212.2 18.5 %attend.5 = (bf16[512,768]{1,0:T(8,128)(2,1)S(1)}, f32[512,768]{1,0:T(8,128)S(1)}) custom-call(s32[2]{0:T(128)S(1)} %and_select_fusion.first_ref, s32[1]{0:T(128)} %constant.65.clone.1.place_ref, bf16[512,768]{1,0:T(8,128)(2,1)S(1)} %get-tuple-element.103.q_ref, bf16[1024,768]{1,0:T(8,128)(2,1)S(1)} %get-tuple-element.95.k_ref, ...), custom_call_target="tpu_custom_call" | custom-call | flops 3221225472 | bytes 12582912 | tf_op jit(solution)/shard_map/attend/pallas_call | solution.py:171
  233.7 5.1 fusion.51
  238.8 2.2 copy-done.43
  241.7 20.5 %multiply_convert_fusion = (bf16[1536,3072]{1,0:T(8,128)(2,1)}, f32[1536,3072]{1,0:T(8,128)}) fusion(f32[3072]{0:T(1024)S(1)} %add.165, bf16[768,3072]{1,0:T(8,128)(2,1)} %all-gather.9.cloned.1.call-done, f32[1536,768]{1,0:T(8,128)} %copy-done.43, f32[768]{0:T(1024)S(1)} %get-tuple-element.78, f32[768]{0:T(1024)S(1)} %get-tuple-element.79, ...), kind=kOutput, calls=%fused_computation.9 | convolution fusion | flops 7300841472 | bytes 37779456 | tf_op jit(solution)/shard_map/dot_general | solution.py:31
  262.2 13.3 %all-gather.11.cloned.1.call-done = bf16[3072,768]{1,0:T(8,128)(2,1)} async-done(((bf16[96,768]{1,0:T(8,128)(2,1)}), bf16[3072,768]{1,0:T(8,128)(2,1)}) %all-gather.11.cloned.1.call-update) | async-done | bytes 4718608 | tf_op jit(solution)/shard_map/all_gather | solution.py:205
  275.5 25.3 %fusion.52 = (bf16[3072]{0:T(1024)(128)(2,1)S(1)}, bf16[1536,3072]{1,0:T(8,128)(2,1)}) fusion(f32[1536,3072]{1,0:T(8,128)} %get-tuple-element.117, f32[3072]{0:T(1024)S(1)} %add.165, bf16[1536,768]{1,0:T(8,128)(2,1)} %bitcast.81, bf16[3072,768]{1,0:T(8,128)(2,1)} %all-gather.11.cloned.1.call-done), kind=kOutput, calls=%fused_computation.149 | convolution fusion | flops 7351563264 | bytes 35407872 | tf_op jit(solution)/shard_map/dot_general | solution.py:39
  300.8 11.1 %multiply_reduce_fusion = (bf16[768]{0:T(1024)(128)(2,1)S(1)}, f32[1536]{0:T(1024)S(1)}, bf16[768]{0:T(1024)(128)(2,1)S(1)}, f32[1536,768]{1,0:T(8,128)S(1)}) fusion(f32[1536,768]{1,0:T(8,128)S(1)} %copy-done.44, f32[1536]{0:T(1024)S(1)} %fusion.39, f32[1536]{0:T(1024)S(1)} %broadcast_multiply_fusion, f32[768]{0:T(1024)S(1)} %get-tuple-element.79, ...), kind=kOutput, calls=%fused_computation.39 | convolution fusion | flops 7257191424 | bytes 23617536 | tf_op jit(solution)/shard_map/dot_general | solution.py:39
  311.9 2.2 fusion.46
  317.7 4.8 convolution_convert_fusion.4
  322.6 14.1 %convolution_convert_fusion.2 = bf16[768,3072]{1,0:T(8,128)(2,1)} fusion(bf16[1536,3072]{1,0:T(8,128)(2,1)} %get-tuple-element.121, f32[1536,768]{1,0:T(8,128)} %copy-done.43, f32[768]{0:T(1024)S(1)} %get-tuple-element.78, f32[768]{0:T(1024)S(1)} %get-tuple-element.79, f32[1536]{0:T(1024)S(1)} %fusion.39, f32[1536]{0:T(1024)S(1)} %broadcast_multiply_fusion), kind=kOutput, calls=%fused_computation.19 | convolution fusion | flops 7256014848 | bytes 18892800 | tf_op jit(solution)/shard_map/dot_general | solution.py:35
  337.1 4.2 convolution_convert_fusion.3
  343.7 20.8 %attend_back.3 = (bf16[512,768]{1,0:T(8,128)(2,1)S(1)}, bf16[1024,768]{1,0:T(8,128)(2,1)S(1)}, bf16[1024,768]{1,0:T(8,128)(2,1)S(1)}) custom-call(s32[2]{0:T(128)S(1)} %and_select_fusion.2.first_ref, s32[1]{0:T(128)} %constant.65.clone.1.place_ref, bf16[512,768]{1,0:T(8,128)(2,1)S(1)} %copy-done.13, bf16[1024,768]{1,0:T(8,128)(2,1)S(1)} %copy-done.7, ...), custom_call_target="tpu_custom_call" | custom-call | flops 9663676416 | bytes 12582912 | tf_op jit(solution)/shard_map/attend_back/pallas_call | solution.py:171
  369.4 20.8 %attend_back.4 = (bf16[512,768]{1,0:T(8,128)(2,1)S(1)}, bf16[1024,768]{1,0:T(8,128)(2,1)S(1)}, bf16[1024,768]{1,0:T(8,128)(2,1)S(1)}) custom-call(s32[2]{0:T(128)S(1)} %and_select_fusion.1.first_ref, s32[1]{0:T(128)} %constant.65.clone.1.place_ref, bf16[512,768]{1,0:T(8,128)(2,1)S(1)} %copy-done.11, bf16[1024,768]{1,0:T(8,128)(2,1)S(1)} %copy-done.3, ...), custom_call_target="tpu_custom_call" | custom-call | flops 9663676416 | bytes 12582912 | tf_op jit(solution)/shard_map/attend_back/pallas_call | solution.py:171
  394.2 20.9 %attend_back.5 = (bf16[512,768]{1,0:T(8,128)(2,1)S(1)}, bf16[1024,768]{1,0:T(8,128)(2,1)S(1)}, bf16[1024,768]{1,0:T(8,128)(2,1)S(1)}) custom-call(s32[2]{0:T(128)S(1)} %and_select_fusion.first_ref, s32[1]{0:T(128)} %constant.65.clone.1.place_ref, bf16[512,768]{1,0:T(8,128)(2,1)S(1)} %copy-done.9, bf16[1024,768]{1,0:T(8,128)(2,1)S(1)} %get-tuple-element.95.k_ref, ...), custom_call_target="tpu_custom_call" | custom-call | flops 9663676416 | bytes 12582912 | tf_op jit(solution)/shard_map/attend_back/pallas_call | solution.py:171
  418.5 9.4 %convolution_convert_fusion = bf16[3072,768]{1,0:T(8,128)(2,1)} fusion(bf16[1536,3072]{1,0:T(8,128)(2,1)S(1)} %bitcast.99, bf16[1536,768]{1,0:T(8,128)(2,1)S(1)} %bitcast.82), kind=kOutput, calls=%fused_computation.17 | convolution fusion | flops 7250116608 | bytes 16515072 | tf_op jit(solution)/shard_map/dot_general | solution.py:35
  429.9 2.5 add_convert_fusion.5
  432.4 4.7 collective-permute-done.4
  437.2 1.8 add_convert_fusion.4
  439.0 26.7 %collective-permute-done.5 = bf16[512,1536]{1,0:T(8,128)(2,1)} collective-permute-done((bf16[512,1536]{1,0:T(8,128)(2,1)}, bf16[512,1536]{1,0:T(8,128)(2,1)}, u32[]{:S(2)}, u32[]{:S(2)}) %collective-permute-start.5) | collective-permute-done | bytes 1572896 | tf_op jit(solution)/shard_map/ppermute | solution.py:316
  465.7 1.8 add_convert_fusion.3
  467.6 32.2 %fusion.45 = (bf16[2304]{0:T(1024)(128)(2,1)S(1)}, bf16[1536,2304]{1,0:T(8,128)(2,1)S(1)}) fusion(bf16[512,1536]{1,0:T(8,128)(2,1)S(1)} %add_convert_fusion.3, bf16[512,1536]{1,0:T(8,128)(2,1)S(1)} %add_convert_fusion.4, bf16[512,1536]{1,0:T(8,128)(2,1)S(1)} %add_convert_fusion.5, bf16[512,768]{1,0:T(8,128)(2,1)S(1)} %copy-done.19, ...), kind=kLoop, calls=%fused_computation.142 | loop fusion | flops 46003968 | bytes 14160384 | tf_op jit(solution)/shard_map/reduce_sum | solution.py:325
  499.9 6.4 fusion.42
  506.3 2.2 copy-done.42
  508.5 2.7 fusion.15
  511.7 9.3 %convolution_convert_fusion.1 = bf16[768,2304]{1,0:T(8,128)(2,1)S(1)} fusion(bf16[1536,768]{1,0:T(8,128)(2,1)} %copy-done.56, bf16[1536,2304]{1,0:T(8,128)(2,1)} %copy-done.51), kind=kOutput, calls=%fused_computation.18 | convolution fusion | flops 5437587456 | bytes 12976128 | tf_op jit(solution)/shard_map/dot_general | solution.py:35
  521.0 2.1 pad_maximum_fusion
  523.1 13.1 %add_convert_fusion = bf16[1536,768]{1,0:T(8,128)(2,1)} fusion(f32[1536,768]{1,0:T(8,128)} %copy-done.43, bf16[1536,3072]{1,0:T(8,128)(2,1)} %get-tuple-element.116, bf16[3072,768]{1,0:T(8,128)(2,1)} %all-gather.11.cloned.1.call-done, f32[768]{0:T(1024)S(1)} %copy-done.70), kind=kOutput, calls=%fused_computation.43 | convolution fusion | flops 7251296256 | bytes 21236736 | tf_op jit(solution)/shard_map/dot_general | solution.py:31
  537.7 8.1 %add_add_fusion.2 = f32[1536,768]{1,0:T(8,128)} fusion(f32[1536,768]{1,0:T(8,128)} %copy-done.38, f32[1536]{0:T(1024)S(1)} %negate_multiply_fusion, f32[1536]{0:T(1024)S(1)} %negate_multiply_fusion.1, bf16[3,512,768]{2,1,0:T(8,128)(2,1)} %param.17, f32[1536]{0:T(1024)S(1)} %multiply_multiply_fusion.2, f32[1536]{0:T(1024)S(1)} %copy-done.59, ...), kind=kLoop, calls=%fused_computation.40 | loop fusion | flops 14155776 | bytes 18908160 | tf_op jit(solution)/shard_map/add | solution.py:329
  545.8 1.6 convert_element_type.152
  547.4 107.2 %reduce-scatter.11.cloned.1.call-done = bf16[96,768]{1,0:T(8,128)(2,1)} async-done(((bf16[3072,768]{1,0:T(8,128)(2,1)}), bf16[96,768]{1,0:T(8,128)(2,1)}) %reduce-scatter.11.cloned.1.call-update) | async-done | bytes 147472 | tf_op jit(solution)/shard_map/reduce_scatter | solution.py:208
  654.7 1.6 convert_element_type.154
  656.3 101.4 %reduce-scatter.13.cloned.1.call-done = bf16[24,2432]{1,0:T(8,128)(2,1)} async-done(((bf16[768,2432]{1,0:T(8,128)(2,1)}), bf16[24,2432]{1,0:T(8,128)(2,1)}) %reduce-scatter.13.cloned.1.call-update) | async-done | bytes 116752
  (255 shorter events, 50.9 us)
Async XLA Ops:
  7.2 67.8 %all-gather.5.cloned.1.call-start = ((), (), s32[]{:S(2)}) async-start(), calls=%async_computation.4 | async-start | bytes 3852288 | tf_op jit(solution)/shard_map/all_gather | solution.py:205
  10.6 223.1 %all-gather.7.cloned.1.call-start = ((), (), s32[]{:S(2)}) async-start(), calls=%async_computation.5 | async-start | bytes 1216512 | tf_op jit(solution)/shard_map/all_gather | solution.py:205
  11.4 230.3 %all-gather.9.cloned.1.call-start = ((), (), s32[]{:S(2)}) async-start(), calls=%async_computation.6 | async-start | bytes 4866048 | tf_op jit(solution)/shard_map/all_gather | solution.py:205
  12.1 263.4 %all-gather.11.cloned.1.call-start = ((), (), s32[]{:S(2)}) async-start(), calls=%async_computation.7 | async-start | bytes 4866048 | tf_op jit(solution)/shard_map/all_gather | solution.py:205
  12.7 523.6 %reduce-scatter.7.cloned.1.call-start = ((), (), s32[]{:S(2)}) async-start(), calls=%async_computation.8 | async-start | bytes 1216512 | tf_op jit(solution)/shard_map/reduce_scatter | solution.py:208
  15.6 64.4 %copy-start.58 = (f32[1536]{0:T(1024)}, f32[1536]{0:T(1024)S(1)}, u32[]{:S(2)}) copy-start(f32[1536]{0:T(1024)S(1)} %div.75) | copy-start | bytes 18436
  15.7 69.6 %copy-start.60 = (f32[1536]{0:T(1024)}, f32[1536]{0:T(1024)S(1)}, u32[]{:S(2)}) copy-start(f32[1536]{0:T(1024)S(1)} %rsqrt.22) | copy-start | bytes 18436
  86.2 10.1 %copy-start.39 = (bf16[3,512,768]{2,1,0:T(8,128)(2,1)S(1)}, bf16[3,512,768]{2,1,0:T(8,128)(2,1)}, u32[]{:S(2)}) copy-start(bf16[3,512,768]{2,1,0:T(8,128)(2,1)} %param.17) | copy-start | bytes 7077892
  88.6 41.5 %collective-permute-start = (bf16[512,1536]{1,0:T(8,128)(2,1)}, bf16[512,1536]{1,0:T(8,128)(2,1)}, u32[]{:S(2)}, u32[]{:S(2)}) collective-permute-start(bf16[512,1536]{1,0:T(8,128)(2,1)} %get-tuple-element.92), channel_id=1, source_target_pairs={{0,1},{2,3},{4,5},{6,7},{8,9},{10,11},{12,13},{14,15},{16,17},{18,... | collective-permute-start | bytes 4718600 | tf_op jit(solution)/shard_map/ppermute | solution.py:240
  93.5 77.2 %copy-start.26 = (s32[512,1]{1,0:T(8,128)}, s32[512,1]{1,0:T(8,128)S(1)}, u32[]{:S(2)}) copy-start(s32[512,1]{1,0:T(8,128)S(1)} %copy.59.q_seg_ref) | copy-start | bytes 6148
  93.8 75.4 %collective-permute-start.1 = (bf16[512,1536]{1,0:T(8,128)(2,1)}, bf16[512,1536]{1,0:T(8,128)(2,1)}, u32[]{:S(2)}, u32[]{:S(2)}) collective-permute-start(bf16[512,1536]{1,0:T(8,128)(2,1)} %get-tuple-element.93), channel_id=1, source_target_pairs={{0,1},{2,3},{4,5},{6,7},{8,9},{10,11},{12,13},{14,15},{16,17},{18,... | collective-permute-start | bytes 4718600 | tf_op jit(solution)/shard_map/ppermute | solution.py:240
  96.4 35.9 %copy-start.28 = (s32[512,1]{1,0:T(8,128)}, s32[512,1]{1,0:T(8,128)S(1)}, u32[]{:S(2)}) copy-start(s32[512,1]{1,0:T(8,128)S(1)} %copy.58.q_seg_ref) | copy-start | bytes 6148
  97.4 113.2 %collective-permute-start.2 = (bf16[512,1536]{1,0:T(8,128)(2,1)}, bf16[512,1536]{1,0:T(8,128)(2,1)}, u32[]{:S(2)}, u32[]{:S(2)}) collective-permute-start(bf16[512,1536]{1,0:T(8,128)(2,1)} %get-tuple-element.91), channel_id=1, source_target_pairs={{0,1},{2,3},{4,5},{6,7},{8,9},{10,11},{12,13},{14,15},{16,17},{18,... | collective-permute-start | bytes 4718600 | tf_op jit(solution)/shard_map/ppermute | solution.py:240
  107.5 43.5 %copy-start.12 = (bf16[512,768]{1,0:T(8,128)(2,1)}, bf16[512,768]{1,0:T(8,128)(2,1)S(1)}, u32[]{:S(2)}) copy-start(bf16[512,768]{1,0:T(8,128)(2,1)S(1)} %get-tuple-element.105.q_ref) | copy-start | bytes 2359300
  107.5 63.3 %copy-start.10 = (bf16[512,768]{1,0:T(8,128)(2,1)}, bf16[512,768]{1,0:T(8,128)(2,1)S(1)}, u32[]{:S(2)}) copy-start(bf16[512,768]{1,0:T(8,128)(2,1)S(1)} %get-tuple-element.104.q_ref) | copy-start | bytes 2359300
  107.5 104.7 %copy-start.8 = (bf16[512,768]{1,0:T(8,128)(2,1)}, bf16[512,768]{1,0:T(8,128)(2,1)S(1)}, u32[]{:S(2)}) copy-start(bf16[512,768]{1,0:T(8,128)(2,1)S(1)} %get-tuple-element.103.q_ref) | copy-start | bytes 2359300
  132.2 18.7 %copy-start.4 = (bf16[1024,768]{1,0:T(8,128)(2,1)}, bf16[1024,768]{1,0:T(8,128)(2,1)S(1)}, u32[]{:S(2)}) copy-start(bf16[1024,768]{1,0:T(8,128)(2,1)S(1)} %get-tuple-element.98.v_ref) | copy-start | bytes 4718596
  132.2 18.7 %copy-start.6 = (bf16[1024,768]{1,0:T(8,128)(2,1)}, bf16[1024,768]{1,0:T(8,128)(2,1)S(1)}, u32[]{:S(2)}) copy-start(bf16[1024,768]{1,0:T(8,128)(2,1)S(1)} %get-tuple-element.99.k_ref) | copy-start | bytes 4718596
  132.3 36.9 %copy-start.53 = (bf16[512,1536]{1,0:T(8,128)(2,1)S(1)}, bf16[512,1536]{1,0:T(8,128)(2,1)}, u32[]{:S(2)}) copy-start(bf16[512,1536]{1,0:T(8,128)(2,1)} %get-tuple-element.93) | copy-start | bytes 4718596
  151.0 19.7 %copy-start.34 = (f32[512,768]{1,0:T(8,128)}, f32[512,768]{1,0:T(8,128)S(1)}, u32[]{:S(2)}) copy-start(f32[512,768]{1,0:T(8,128)S(1)} %get-tuple-element.26.lse_ref) | copy-start | bytes 4718596
  151.0 38.3 %copy-start.24 = (bf16[512,768]{1,0:T(8,128)(2,1)}, bf16[512,768]{1,0:T(8,128)(2,1)S(1)}, u32[]{:S(2)}) copy-start(bf16[512,768]{1,0:T(8,128)(2,1)S(1)} %get-tuple-element.23.o_ref) | copy-start | bytes 2359300
  170.7 18.6 %copy-start = (bf16[1024,768]{1,0:T(8,128)(2,1)}, bf16[1024,768]{1,0:T(8,128)(2,1)S(1)}, u32[]{:S(2)}) copy-start(bf16[1024,768]{1,0:T(8,128)(2,1)S(1)} %get-tuple-element.96.v_ref) | copy-start | bytes 4718596
  170.7 18.6 %copy-start.2 = (bf16[1024,768]{1,0:T(8,128)(2,1)}, bf16[1024,768]{1,0:T(8,128)(2,1)S(1)}, u32[]{:S(2)}) copy-start(bf16[1024,768]{1,0:T(8,128)(2,1)S(1)} %get-tuple-element.97.k_ref) | copy-start | bytes 4718596
  170.8 39.8 %copy-start.52 = (bf16[512,1536]{1,0:T(8,128)(2,1)S(1)}, bf16[512,1536]{1,0:T(8,128)(2,1)}, u32[]{:S(2)}) copy-start(bf16[512,1536]{1,0:T(8,128)(2,1)} %get-tuple-element.91) | copy-start | bytes 4718596
  189.3 22.9 %copy-start.32 = (f32[512,768]{1,0:T(8,128)}, f32[512,768]{1,0:T(8,128)S(1)}, u32[]{:S(2)}) copy-start(f32[512,768]{1,0:T(8,128)S(1)} %get-tuple-element.28.lse_ref) | copy-start | bytes 4718596
  189.3 41.4 %copy-start.22 = (bf16[512,768]{1,0:T(8,128)(2,1)}, bf16[512,768]{1,0:T(8,128)(2,1)S(1)}, u32[]{:S(2)}) copy-start(bf16[512,768]{1,0:T(8,128)(2,1)S(1)} %get-tuple-element.24.o_ref) | copy-start | bytes 2359300
  275.5 25.3 %copy-start.44 = (f32[1536,768]{1,0:T(8,128)S(1)}, f32[1536,768]{1,0:T(8,128)}, u32[]{:S(2)}) copy-start(f32[1536,768]{1,0:T(8,128)} %copy-done.43) | copy-start | bytes 14155780
  275.5 25.3 %copy-start.71 = (bf16[768,3072]{1,0:T(8,128)(2,1)S(1)}, bf16[768,3072]{1,0:T(8,128)(2,1)}, u32[]{:S(2)}) copy-start(bf16[768,3072]{1,0:T(8,128)(2,1)} %all-gather.9.cloned.1.call-done) | copy-start | bytes 14155780
  322.5 223.3 %reduce-scatter.9.cloned.1.call-start = ((), (), s32[]{:S(2)}) async-start(), calls=%async_computation.9 | async-start | bytes 4866048 | tf_op jit(solution)/shard_map/reduce_scatter | solution.py:208
  336.6 318.0 %reduce-scatter.11.cloned.1.call-start = ((), (), s32[]{:S(2)}) async-start(), calls=%async_computation.10 | async-start | bytes 4866048 | tf_op jit(solution)/shard_map/reduce_scatter | solution.py:208
  364.8 25.4 %copy-start.45 = (bf16[1024,1536]{1,0:T(8,128)(2,1)}, bf16[1024,1536]{1,0:T(8,128)(2,1)S(1)}, u32[]{:S(2)}) copy-start(bf16[1024,1536]{1,0:T(8,128)(2,1)S(1)} %constant_dynamic-update-slice_fusion.3) | copy-start | bytes 9437188
  366.1 62.4 %collective-permute-start.3 = (bf16[512,1536]{1,0:T(8,128)(2,1)}, bf16[512,1536]{1,0:T(8,128)(2,1)}, u32[]{:S(2)}, u32[]{:S(2)}) collective-permute-start(bf16[512,1536]{1,0:T(8,128)(2,1)} %slice.261), channel_id=1, source_target_pairs={{1,0},{3,2},{5,4},{7,6},{9,8},{11,10},{13,12},{15,14},{17,16},{19,... | collective-permute-start | bytes 4718600 | tf_op jit(solution)/shard_map/ppermute | solution.py:316
  390.5 27.8 %slice-start = ((s8[9437184]{0:T(1024)(128)(4,1)}), s8[1048576]{0:T(1024)(128)(4,1)S(1)}, s32[]{:S(2)}) async-start(s8[9437184]{0:T(1024)(128)(4,1)} %bitcast.98), calls=%async_computation.12 | async-start | bytes 2097152
  391.9 45.3 %collective-permute-start.4 = (bf16[512,1536]{1,0:T(8,128)(2,1)}, bf16[512,1536]{1,0:T(8,128)(2,1)}, u32[]{:S(2)}, u32[]{:S(2)}) collective-permute-start(bf16[512,1536]{1,0:T(8,128)(2,1)} %slice.263), channel_id=1, source_target_pairs={{1,0},{3,2},{5,4},{7,6},{9,8},{11,10},{13,12},{15,14},{17,16},{19,... | collective-permute-start | bytes 4718600 | tf_op jit(solution)/shard_map/ppermute | solution.py:316
  394.2 24.0 %slice-start.1 = ((s8[9437184]{0:T(1024)(128)(4,1)}), s8[4194304]{0:T(1024)(128)(4,1)S(1)}, s32[]{:S(2)}) async-start(s8[9437184]{0:T(1024)(128)(4,1)} %bitcast.98), calls=%async_computation.13 | async-start | bytes 8388608
  394.2 24.0 %slice-start.2 = ((s8[9437184]{0:T(1024)(128)(4,1)}), s8[4194304]{0:T(1024)(128)(4,1)S(1)}, s32[]{:S(2)}) async-start(s8[9437184]{0:T(1024)(128)(4,1)} %bitcast.98), calls=%async_computation.14 | async-start | bytes 8388608
  416.7 49.0 %collective-permute-start.5 = (bf16[512,1536]{1,0:T(8,128)(2,1)}, bf16[512,1536]{1,0:T(8,128)(2,1)}, u32[]{:S(2)}, u32[]{:S(2)}) collective-permute-start(bf16[512,1536]{1,0:T(8,128)(2,1)} %slice.265), channel_id=1, source_target_pairs={{1,0},{3,2},{5,4},{7,6},{9,8},{11,10},{13,12},{15,14},{17,16},{19,... | collective-permute-start | bytes 4718600 | tf_op jit(solution)/shard_map/ppermute | solution.py:316
  428.5 329.3 %reduce-scatter.13.cloned.1.call-start = ((), (), s32[]{:S(2)}) async-start(), calls=%async_computation.11 | async-start | bytes 3852288
  428.5 8.7 %copy-start.48 = (bf16[1024,1536]{1,0:T(8,128)(2,1)S(1)}, bf16[1024,1536]{1,0:T(8,128)(2,1)}, u32[]{:S(2)}) copy-start(bf16[1024,1536]{1,0:T(8,128)(2,1)} %copy-done.47) | copy-start | bytes 9437188
  428.5 37.1 %copy-start.50 = (bf16[1024,1536]{1,0:T(8,128)(2,1)S(1)}, bf16[1024,1536]{1,0:T(8,128)(2,1)}, u32[]{:S(2)}) copy-start(bf16[1024,1536]{1,0:T(8,128)(2,1)} %copy-done.49) | copy-start | bytes 9437188
  432.4 35.1 %copy-start.15 = (bf16[512,768]{1,0:T(8,128)(2,1)S(1)}, bf16[512,768]{1,0:T(8,128)(2,1)}, u32[]{:S(2)}) copy-start(bf16[512,768]{1,0:T(8,128)(2,1)} %copy-done.14) | copy-start | bytes 2359300
  432.4 35.1 %copy-start.17 = (bf16[512,768]{1,0:T(8,128)(2,1)S(1)}, bf16[512,768]{1,0:T(8,128)(2,1)}, u32[]{:S(2)}) copy-start(bf16[512,768]{1,0:T(8,128)(2,1)} %copy-done.16) | copy-start | bytes 2359300
  432.4 35.1 %copy-start.19 = (bf16[512,768]{1,0:T(8,128)(2,1)S(1)}, bf16[512,768]{1,0:T(8,128)(2,1)}, u32[]{:S(2)}) copy-start(bf16[512,768]{1,0:T(8,128)(2,1)} %copy-done.18) | copy-start | bytes 2359300
  467.5 32.3 %copy-start.37 = (bf16[3,512,768]{2,1,0:T(8,128)(2,1)S(1)}, bf16[3,512,768]{2,1,0:T(8,128)(2,1)}, u32[]{:S(2)}) copy-start(bf16[3,512,768]{2,1,0:T(8,128)(2,1)} %param.9) | copy-start | bytes 7077892
  467.5 32.3 %copy-start.59 = (f32[1536]{0:T(1024)S(1)}, f32[1536]{0:T(1024)}, u32[]{:S(2)}) copy-start(f32[1536]{0:T(1024)} %copy-done.58) | copy-start | bytes 18436
  467.5 32.3 %copy-start.65 = (f32[768]{0:T(1024)S(1)}, f32[768]{0:T(1024)}, u32[]{:S(2)}) copy-start(f32[768]{0:T(1024)} %copy-done.64) | copy-start | bytes 9220
  467.5 32.3 %copy-start.69 = (bf16[768,2432]{1,0:T(8,128)(2,1)S(1)}, bf16[768,2432]{1,0:T(8,128)(2,1)}, u32[]{:S(2)}) copy-start(bf16[768,2432]{1,0:T(8,128)(2,1)} %all-gather.5.cloned.1.call-done) | copy-start | bytes 11206660
  499.9 8.6 %copy-start.61 = (f32[1536]{0:T(1024)S(1)}, f32[1536]{0:T(1024)}, u32[]{:S(2)}) copy-start(f32[1536]{0:T(1024)} %copy-done.60) | copy-start | bytes 18436
  (41 other events, 130.8 us)
Sparse Core Ops, SparseCore 0:
  11.5 63.4 all-gather.4
  77.9 53.7 all-gather.6
  134.7 66.8 all-gather.8
  204.3 71.1 all-gather.10
  322.6 100.5 reduce-scatter.6
  428.5 113.6 reduce-scatter.8
  548.6 106.0 reduce-scatter.10
  660.3 97.3 reduce-scatter.12

commit v2 on v1

--- a/solution.py
+++ b/solution.py
@@ -213,9 +213,13 @@
     extra = jnp.concatenate([vectors.T, up_bias.reshape(row_share, bias_count)], 1)
     extra = jnp.pad(extra, ((0, 0), (0, LANES - extra_count)))
     wide = gather(jnp.concatenate([qkv_weight, extra], 1))
-    w_out = gather(out_weight)
-    w_up = gather(up_weight)
-    w_down = gather(down_weight)
+    units = up_weight.shape[1]
+    rest = gather(
+        jnp.concatenate([out_weight, up_weight, down_weight.reshape(row_share, units)], 1)
+    )
+    w_out = rest[:, :width]
+    w_up = rest[:, width : width + units]
+    w_down = rest[:, width + units :].reshape(units, width)
     w_qkv = wide[:, : 3 * width]
     small = wide[:, 3 * width : 3 * width + extra_count].astype(F32)
     vec_rows = small[:, :vec_count].T
@@ -279,18 +283,19 @@
 
     grad_low = cotangent.reshape(micro_count * span_rows, width)
     grad_rows = grad_low.astype(F32)
-    own_down = scatter(contract_rows(active, grad_low))
+    grad_down = contract_rows(active, grad_low).astype(BF16).reshape(width, units)
     grad_bdown = jnp.sum(grad_rows, 0)
     grad_act = contract_cols(grad_low, w_down)
     grad_pre = jax.vjp(gelu_tanh, pre_act)[1](grad_act)[0].astype(BF16)
-    own_up = scatter(contract_rows(inner, grad_pre))
+    grad_up = contract_rows(inner, grad_pre).astype(BF16)
+    own_feed = scatter(jnp.concatenate([grad_up, grad_down], 1)).astype(F32)
     grad_bias = jnp.sum(grad_pre.astype(F32), 0)
     grad_inner = contract_cols(grad_pre, w_up)
     norm_two_back = jax.vjp(layer_norm, middle, vec_rows[5], vec_rows[6])[1]
     grad_mid_norm, grad_gain_two, grad_shift_two = norm_two_back(grad_inner)
     grad_middle = grad_rows + grad_mid_norm
     grad_branch = grad_middle.astype(BF16)
-    own_out = scatter(contract_rows(attended, grad_branch))
+    grad_out = contract_rows(attended, grad_branch)
     grad_bout = jnp.sum(grad_branch.astype(F32), 0)
     grad_att = contract_cols(grad_branch, w_out).astype(BF16)
     grad_att = grad_att.reshape(micro_count, span_rows, width)
@@ -322,7 +327,7 @@
     grad_kv = jnp.concatenate(grad_kvs, 0)
     grad_mixed = jnp.concatenate([grad_query, grad_kv], 1)
     grad_qkv = contract_rows(hidden, grad_mixed)
-    column_sums = jnp.sum(grad_mixed.astype(F32), 0)
+    column_sums = dot(jnp.ones((8, grad_mixed.shape[0]), BF16), grad_mixed)[0]
     grad_hidden = contract_cols(grad_mixed, w_qkv)
     norm_one_back = jax.vjp(layer_norm, token_rows, vec_rows[0], vec_rows[1])[1]
     grad_tok_norm, grad_gain_one, grad_shift_one = norm_one_back(grad_hidden)
@@ -341,15 +346,15 @@
     )
     grad_extra = jnp.concatenate([grad_vec.T, grad_bias.reshape(width, bias_count)], 1)
     grad_extra = jnp.pad(grad_extra, ((0, 0), (0, LANES - extra_count)))
-    own_wide = scatter(jnp.concatenate([grad_qkv, grad_extra], 1)).astype(F32)
-    own_small = own_wide[:, 3 * width : 3 * width + extra_count]
+    own_wide = scatter(jnp.concatenate([grad_qkv, grad_out, grad_extra], 1)).astype(F32)
+    own_small = own_wide[:, 4 * width : 4 * width + extra_count]
     return (
         result.reshape(tokens.shape),
         input_grad.reshape(tokens.shape),
         own_wide[:, : 3 * width],
-        own_out.astype(F32),
-        own_up.astype(F32),
-        own_down.astype(F32),
+        own_wide[:, 3 * width : 4 * width],
+        own_feed[:, :units],
+        own_feed[:, units:].reshape(down_weight.shape),
         own_small[:, :vec_count].T,
         own_small[:, vec_count:].reshape(-1),
     )

time: 776 us -> 823 us (1.061); the launches traced: 769 us -> 807 us
  local copies, waits for them, and re-layouts: 37.2 us -> 70.5 us
    unnamed x9 -> x5, waiting for transfers between devices: 103 us -> 51.7 us
    concatenate x1 -> x4, other arithmetic: 2.07 us -> 42.4 us  [the longest x1 31.8 us: on_device(): grad_mixed = jnp.concatenate([grad_query, grad_kv], 1)]
    reduce_sum x1 -> x0, other arithmetic: 32.2 us -> none  [on_device(): column_sums = jnp.sum(grad_mixed.astype(F32), 0)]
    reduce_scatter x3 -> x1, waiting for transfers between devices: 107 us -> 135 us  [scatter(): lax.psum_scatter(whole.astype(BF16), both, scatter_dimension=0, tiled=True)]
    ppermute x3, waiting for transfers between devices: 31.4 us -> 56.2 us  [on_device(): theirs = lax.ppermute(kv_terms[:span_rows], 'ctx', [(1, 0)])]
    reshape x0 -> x4, local copies, waits for them, and re-layouts: none -> 19 us  [the longest x1 8.74 us: on_device(): contract_rows(active, grad_low).astype(BF16).reshape(width, units)]
    all_gather x4 -> x2, waiting for transfers between devices: 71.6 us -> 57.6 us  [gather(): return lax.all_gather(shard, both, axis=0, tiled=True)]
    ppermute x3, waiting for transfers between devices: 60 us -> 71.3 us  [on_device(): before = lax.ppermute(own_kv, 'ctx', [(0, 1)])]
  transfers between devices with their start and end apart: 14 -> 10, of which waited for: 9 -> 8; matrix products, arithmetic and copies ran while one was open for 23% -> 14% of each run, Pallas kernels for 15% -> 12%
where the time goes in v2:
time: 823 us; the launch traced here: 807 us
  waiting for transfers between devices  372 us (45%)
  matrix products  134 us (16%)
  Pallas kernels  118 us (14%)
  other arithmetic  82.9 us (10%)
  local copies, waits for them, and re-layouts  70.5 us (9%)
  between operations  15.3 us (2%)
  starting transfers between devices  14.2 us (2%)
    reduce_scatter x1, waiting for transfers between devices, scatter(): lax.psum_scatter(whole.astype(BF16), both, scatter_dimension=0, tiled=True)  135 us
    pallas_call x6, Pallas kernels, attention_call(): pl.pallas_call(kernel, grid_spec=pltpu.PrefetchScalarGridSpec(num_scalar_...  118 us
    ppermute x3, waiting for transfers between devices, on_device(): before = lax.ppermute(own_kv, 'ctx', [(0, 1)])  71.3 us
    all_gather x2, waiting for transfers between devices, gather(): return lax.all_gather(shard, both, axis=0, tiled=True)  57.6 us
    ppermute x3, waiting for transfers between devices, on_device(): theirs = lax.ppermute(kv_terms[:span_rows], 'ctx', [(1, 0)])  56.2 us
    unnamed x5, waiting for transfers between devices  51.7 us
    dot_general x6, matrix products, dot(): return jnp.dot(left, right, preferred_element_type=F32)  49.1 us
    dot_general x4, matrix products, contract_cols(): lax.dot_general(left, right, (((1,), (1,)), ((), ())), preferred_element_...  45.9 us
  transfers between devices with their start and end apart: 10, of which 8 were waited for; matrix products, arithmetic and copies ran while one was open for 14% of the time, Pallas kernels for 12%

profile of v2, /device:TPU:0, one launch (start us, length us, event | category | flops | bytes accessed | tf_op | source)
XLA Modules:
  0.0 807.0 jit_solution(2228893329550842477)
XLA Ops:
  13.4 2.0 convert_reduce_fusion
  17.4 57.6 %all-gather.3.cloned.1.call-done = bf16[768,2432]{1,0:T(8,128)(2,1)} async-done(((bf16[24,2432]{1,0:T(8,128)(2,1)}), bf16[768,2432]{1,0:T(8,128)(2,1)}) %all-gather.3.cloned.1.call-update) | async-done | bytes 3735568 | tf_op jit(solution)/shard_map/all_gather | solution.py:205
  81.5 3.8 fusion.30
  86.3 2.4 pad_maximum_fusion.3
  88.7 4.5 collective-permute-start
  93.8 2.5 collective-permute-start.1
  97.5 2.5 collective-permute-start.2
  99.9 5.4 add_convert_fusion.2
  105.8 1.8 fusion.57
  107.6 29.0 %collective-permute-done = bf16[512,1536]{1,0:T(8,128)(2,1)} collective-permute-done((bf16[512,1536]{1,0:T(8,128)(2,1)}, bf16[512,1536]{1,0:T(8,128)(2,1)}, u32[]{:S(2)}, u32[]{:S(2)}) %collective-permute-start) | collective-permute-done | bytes 1572896 | tf_op jit(solution)/shard_map/ppermute | solution.py:244
  136.5 2.4 pad_maximum_fusion.5
  138.9 18.6 %attend.3 = (bf16[512,768]{1,0:T(8,128)(2,1)S(1)}, f32[512,768]{1,0:T(8,128)S(1)}) custom-call(s32[2]{0:T(128)S(1)} %and_select_fusion.2.first_ref, s32[1]{0:T(128)} %constant.66.clone.1.place_ref, bf16[512,768]{1,0:T(8,128)(2,1)S(1)} %get-tuple-element.103.q_ref, bf16[1024,768]{1,0:T(8,128)(2,1)S(1)} %get-tuple-element.97.k_ref, ...), custom_call_target="tpu_custom_call" | custom-call | flops 3221225472 | bytes 12582912 | tf_op jit(solution)/shard_map/attend/pallas_call | solution.py:171
  158.7 30.5 %collective-permute-done.1 = bf16[512,1536]{1,0:T(8,128)(2,1)} collective-permute-done((bf16[512,1536]{1,0:T(8,128)(2,1)}, bf16[512,1536]{1,0:T(8,128)(2,1)}, u32[]{:S(2)}, u32[]{:S(2)}) %collective-permute-start.1) | collective-permute-done | bytes 1572896 | tf_op jit(solution)/shard_map/ppermute | solution.py:244
  190.8 18.5 %attend.4 = (bf16[512,768]{1,0:T(8,128)(2,1)S(1)}, f32[512,768]{1,0:T(8,128)S(1)}) custom-call(s32[2]{0:T(128)S(1)} %and_select_fusion.1.first_ref, s32[1]{0:T(128)} %constant.66.clone.1.place_ref, bf16[512,768]{1,0:T(8,128)(2,1)S(1)} %get-tuple-element.102.q_ref, bf16[1024,768]{1,0:T(8,128)(2,1)S(1)} %get-tuple-element.95.k_ref, ...), custom_call_target="tpu_custom_call" | custom-call | flops 3221225472 | bytes 12582912 | tf_op jit(solution)/shard_map/attend/pallas_call | solution.py:171
  210.4 11.9 %collective-permute-done.2 = bf16[512,1536]{1,0:T(8,128)(2,1)} collective-permute-done((bf16[512,1536]{1,0:T(8,128)(2,1)}, bf16[512,1536]{1,0:T(8,128)(2,1)}, u32[]{:S(2)}, u32[]{:S(2)}) %collective-permute-start.2) | collective-permute-done | bytes 1572896 | tf_op jit(solution)/shard_map/ppermute | solution.py:244
  223.8 18.5 %attend.5 = (bf16[512,768]{1,0:T(8,128)(2,1)S(1)}, f32[512,768]{1,0:T(8,128)S(1)}) custom-call(s32[2]{0:T(128)S(1)} %and_select_fusion.first_ref, s32[1]{0:T(128)} %constant.66.clone.1.place_ref, bf16[512,768]{1,0:T(8,128)(2,1)S(1)} %get-tuple-element.101.q_ref, bf16[1024,768]{1,0:T(8,128)(2,1)S(1)} %get-tuple-element.93.k_ref, ...), custom_call_target="tpu_custom_call" | custom-call | flops 3221225472 | bytes 12582912 | tf_op jit(solution)/shard_map/attend/pallas_call | solution.py:171
  245.4 5.1 fusion.61
  250.5 2.2 copy-done.43
  253.3 4.8 slice.287
  258.1 8.5 %reshape.189 = bf16[3072,768]{1,0:T(8,128)(2,1)} reshape(bf16[768,3072]{1,0:T(8,128)(2,1)} %slice.287) | data formatting | bytes 9437184 | tf_op jit(solution)/shard_map/reshape | solution.py:222
  266.6 20.4 %multiply_convert_fusion = (bf16[1536,3072]{1,0:T(8,128)(2,1)}, f32[1536,3072]{1,0:T(8,128)}) fusion(f32[3072]{0:T(1024)S(1)} %add.161, bf16[768,6912]{1,0:T(8,128)(2,1)} %all-gather.5.cloned.1.call-done, f32[1536,768]{1,0:T(8,128)} %copy-done.43, f32[768]{0:T(1024)S(1)} %get-tuple-element.78, f32[768]{0:T(1024)S(1)} %get-tuple-element.79, ...), kind=kOutput, calls=%fused_computation.14 | convolution fusion | flops 7300841472 | bytes 37779456 | tf_op jit(solution)/shard_map/dot_general | solution.py:31
  287.0 23.2 %fusion.62 = (bf16[3072]{0:T(1024)(128)(2,1)S(1)}, bf16[1536,3072]{1,0:T(8,128)(2,1)}) fusion(f32[1536,3072]{1,0:T(8,128)} %get-tuple-element.117, f32[3072]{0:T(1024)S(1)} %add.161, bf16[3072,768]{1,0:T(8,128)(2,1)} %reshape.189, bf16[1536,768]{1,0:T(8,128)(2,1)S(1)} %bitcast.92), kind=kOutput, calls=%fused_computation.164 | convolution fusion | flops 7351563264 | bytes 35407872 | tf_op jit(solution)/shard_map/dot_general | solution.py:39
  310.2 12.8 %multiply_reduce_fusion = (bf16[768]{0:T(1024)(128)(2,1)S(1)}, f32[1536]{0:T(1024)S(1)}, bf16[768]{0:T(1024)(128)(2,1)S(1)}, f32[1536,768]{1,0:T(8,128)S(1)}) fusion(f32[1536,768]{1,0:T(8,128)S(1)} %bitcast.94, f32[1536]{0:T(1024)S(1)} %fusion.49, f32[1536]{0:T(1024)S(1)} %broadcast_multiply_fusion, f32[768]{0:T(1024)S(1)} %get-tuple-element.79, ...), kind=kOutput, calls=%fused_computation.46 | convolution fusion | flops 7257191424 | bytes 23617536 | tf_op jit(solution)/shard_map/dot_general | solution.py:39
  323.1 3.8 fusion.55
  330.4 3.4 convolution_convert_fusion.3
  336.2 20.8 %attend_back.3 = (bf16[512,768]{1,0:T(8,128)(2,1)S(1)}, bf16[1024,768]{1,0:T(8,128)(2,1)S(1)}, bf16[1024,768]{1,0:T(8,128)(2,1)S(1)}) custom-call(s32[2]{0:T(128)S(1)} %and_select_fusion.2.first_ref, s32[1]{0:T(128)} %constant.66.clone.1.place_ref, bf16[512,768]{1,0:T(8,128)(2,1)S(1)} %copy-done.15, bf16[1024,768]{1,0:T(8,128)(2,1)S(1)} %copy-done.7, ...), custom_call_target="tpu_custom_call" | custom-call | flops 9663676416 | bytes 12582912 | tf_op jit(solution)/shard_map/attend_back/pallas_call | solution.py:171
  362.0 21.0 %attend_back.4 = (bf16[512,768]{1,0:T(8,128)(2,1)S(1)}, bf16[1024,768]{1,0:T(8,128)(2,1)S(1)}, bf16[1024,768]{1,0:T(8,128)(2,1)S(1)}) custom-call(s32[2]{0:T(128)S(1)} %and_select_fusion.1.first_ref, s32[1]{0:T(128)} %constant.66.clone.1.place_ref, bf16[512,768]{1,0:T(8,128)(2,1)S(1)} %copy-done.11, bf16[1024,768]{1,0:T(8,128)(2,1)S(1)} %copy-done.3, ...), custom_call_target="tpu_custom_call" | custom-call | flops 9663676416 | bytes 12582912 | tf_op jit(solution)/shard_map/attend_back/pallas_call | solution.py:171
  386.9 20.9 %attend_back.5 = (bf16[512,768]{1,0:T(8,128)(2,1)S(1)}, bf16[1024,768]{1,0:T(8,128)(2,1)S(1)}, bf16[1024,768]{1,0:T(8,128)(2,1)S(1)}) custom-call(s32[2]{0:T(128)S(1)} %and_select_fusion.first_ref, s32[1]{0:T(128)} %constant.66.clone.1.place_ref, bf16[512,768]{1,0:T(8,128)(2,1)S(1)} %copy-done.9, bf16[1024,768]{1,0:T(8,128)(2,1)S(1)} %get-tuple-element.93.k_ref, ...), custom_call_target="tpu_custom_call" | custom-call | flops 9663676416 | bytes 12582912 | tf_op jit(solution)/shard_map/attend_back/pallas_call | solution.py:171
  413.8 5.6 convolution_convert_fusion.5
  419.4 1.9 add_convert_fusion.5
  421.4 29.5 %collective-permute-done.4 = bf16[512,1536]{1,0:T(8,128)(2,1)} collective-permute-done((bf16[512,1536]{1,0:T(8,128)(2,1)}, bf16[512,1536]{1,0:T(8,128)(2,1)}, u32[]{:S(2)}, u32[]{:S(2)}) %collective-permute-start.4) | collective-permute-done | bytes 1572896 | tf_op jit(solution)/shard_map/ppermute | solution.py:321
  450.9 1.8 add_convert_fusion.4
  452.7 26.6 %collective-permute-done.5 = bf16[512,1536]{1,0:T(8,128)(2,1)} collective-permute-done((bf16[512,1536]{1,0:T(8,128)(2,1)}, bf16[512,1536]{1,0:T(8,128)(2,1)}, u32[]{:S(2)}, u32[]{:S(2)}) %collective-permute-start.5) | collective-permute-done | bytes 1572896 | tf_op jit(solution)/shard_map/ppermute | solution.py:321
  479.4 1.8 add_convert_fusion.3
  481.2 31.8 %maximum_maximum_fusion = bf16[1536,2304]{1,0:T(8,128)(2,1)S(1)} fusion(bf16[512,1536]{1,0:T(8,128)(2,1)S(1)} %add_convert_fusion.3, bf16[512,1536]{1,0:T(8,128)(2,1)S(1)} %add_convert_fusion.4, bf16[512,1536]{1,0:T(8,128)(2,1)S(1)} %add_convert_fusion.5, bf16[512,768]{1,0:T(8,128)(2,1)S(1)} %copy-done.19, bf16[512,768]{1,0:T(8,128)(2,1)S(1)} %copy-done.17, ...), kind=kLoop, calls=%fused_computation.16 | loop fusion | flops 42467328 | bytes 14155776 | tf_op jit(solution)/shard_map/concatenate | solution.py:328
  514.7 7.5 convolution_convert_fusion.1
  522.3 6.4 fusion.52
  528.7 2.1 copy-done.42
  530.8 3.1 fusion.18
  539.8 4.9 pad_maximum_fusion.1
  544.7 12.4 %convolution_convert_fusion = bf16[3072,768]{1,0:T(8,128)(2,1)} fusion(bf16[1536,3072]{1,0:T(8,128)(2,1)} %get-tuple-element.116, bf16[1536,768]{1,0:T(8,128)(2,1)} %bitcast.91), kind=kOutput, calls=%fused_computation.23 | convolution fusion | flops 7250116608 | bytes 16515072 | tf_op jit(solution)/shard_map/dot_general | solution.py:35
  557.2 8.7 %reshape.198 = bf16[768,3072]{1,0:T(8,128)(2,1)} reshape(bf16[3072,768]{1,0:T(8,128)(2,1)} %convolution_convert_fusion) | data formatting | bytes 9437184 | tf_op jit(solution)/shard_map/reshape | solution.py:286
  565.9 13.0 %convolution_convert_fusion.2 = bf16[768,3072]{1,0:T(8,128)(2,1)S(1)} fusion(bf16[1536,3072]{1,0:T(8,128)(2,1)} %get-tuple-element.121, f32[1536,768]{1,0:T(8,128)} %copy-done.43, f32[768]{0:T(1024)S(1)} %copy-done.84, f32[768]{0:T(1024)S(1)} %copy-done.79, f32[1536]{0:T(1024)S(1)} %copy-done.75, f32[1536]{0:T(1024)S(1)} %copy-done.68), kind=kOutput, calls=%fused_computation.25 | convolution fusion | flops 7256014848 | bytes 18892800 | tf_op jit(solution)/shard_map/dot_general | solution.py:35
  579.0 4.1 pad_maximum_fusion
  583.8 13.4 %add_convert_fusion = bf16[1536,768]{1,0:T(8,128)(2,1)} fusion(f32[1536,768]{1,0:T(8,128)} %copy-done.43, bf16[1536,3072]{1,0:T(8,128)(2,1)} %get-tuple-element.116, bf16[3072,768]{1,0:T(8,128)(2,1)} %reshape.189, f32[768]{0:T(1024)S(1)} %copy-done.82), kind=kOutput, calls=%fused_computation.50 | convolution fusion | flops 7251296256 | bytes 21236736 | tf_op jit(solution)/shard_map/dot_general | solution.py:31
  597.2 7.6 add_add_fusion.2
  604.8 51.6 %reduce-scatter.7.cloned.1.call-done = bf16[24,3200]{1,0:T(8,128)(2,1)} async-done(((bf16[768,3200]{1,0:T(8,128)(2,1)}), bf16[24,3200]{1,0:T(8,128)(2,1)}) %reduce-scatter.7.cloned.1.call-update) | async-done | bytes 153616
  662.4 135.4 %reduce-scatter.5.cloned.1.call-done = bf16[24,6144]{1,0:T(8,128)(2,1)} async-done(((bf16[768,6144]{1,0:T(8,128)(2,1)}), bf16[24,6144]{1,0:T(8,128)(2,1)}) %reduce-scatter.5.cloned.1.call-update) | async-done | bytes 294928 | tf_op jit(solution)/shard_map/reduce_scatter | solution.py:208
  (272 shorter events, 63.6 us)
Async XLA Ops:
  7.2 67.8 %all-gather.3.cloned.1.call-start = ((), (), s32[]{:S(2)}) async-start(), calls=%async_computation.2 | async-start | bytes 3852288 | tf_op jit(solution)/shard_map/all_gather | solution.py:205
  10.6 234.7 %all-gather.5.cloned.1.call-start = ((), (), s32[]{:S(2)}) async-start(), calls=%async_computation.3 | async-start | bytes 10948608 | tf_op jit(solution)/shard_map/all_gather | solution.py:205
  13.4 643.0 %reduce-scatter.7.cloned.1.call-start = ((), (), s32[]{:S(2)}) async-start(), calls=%async_computation.5 | async-start | bytes 5068800
  15.5 64.5 %copy-start.59 = (f32[1536]{0:T(1024)}, f32[1536]{0:T(1024)S(1)}, u32[]{:S(2)}) copy-start(f32[1536]{0:T(1024)S(1)} %div.75) | copy-start | bytes 18436
  16.4 68.9 %copy-start.61 = (f32[1536]{0:T(1024)}, f32[1536]{0:T(1024)S(1)}, u32[]{:S(2)}) copy-start(f32[1536]{0:T(1024)S(1)} %rsqrt.22) | copy-start | bytes 18436
  78.5 188.1 %copy-start.83 = (f32[768]{0:T(1024)}, f32[768]{0:T(1024)S(1)}, u32[]{:S(2)}) copy-start(f32[768]{0:T(1024)S(1)} %get-tuple-element.78) | copy-start | bytes 9220
  78.5 244.6 %copy-start.78 = (f32[768]{0:T(1024)}, f32[768]{0:T(1024)S(1)}, u32[]{:S(2)}) copy-start(f32[768]{0:T(1024)S(1)} %get-tuple-element.79) | copy-start | bytes 9220
  88.7 47.9 %collective-permute-start = (bf16[512,1536]{1,0:T(8,128)(2,1)}, bf16[512,1536]{1,0:T(8,128)(2,1)}, u32[]{:S(2)}, u32[]{:S(2)}) collective-permute-start(bf16[512,1536]{1,0:T(8,128)(2,1)} %get-tuple-element.90), channel_id=1, source_target_pairs={{0,1},{2,3},{4,5},{6,7},{8,9},{10,11},{12,13},{14,15},{16,17},{18,... | collective-permute-start | bytes 4718600 | tf_op jit(solution)/shard_map/ppermute | solution.py:244
  93.6 97.2 %copy-start.26 = (s32[512,1]{1,0:T(8,128)}, s32[512,1]{1,0:T(8,128)S(1)}, u32[]{:S(2)}) copy-start(s32[512,1]{1,0:T(8,128)S(1)} %copy.62.q_seg_ref) | copy-start | bytes 6148
  93.8 95.4 %collective-permute-start.1 = (bf16[512,1536]{1,0:T(8,128)(2,1)}, bf16[512,1536]{1,0:T(8,128)(2,1)}, u32[]{:S(2)}, u32[]{:S(2)}) collective-permute-start(bf16[512,1536]{1,0:T(8,128)(2,1)} %get-tuple-element.91), channel_id=1, source_target_pairs={{0,1},{2,3},{4,5},{6,7},{8,9},{10,11},{12,13},{14,15},{16,17},{18,... | collective-permute-start | bytes 4718600 | tf_op jit(solution)/shard_map/ppermute | solution.py:244
  96.4 42.5 %copy-start.28 = (s32[512,1]{1,0:T(8,128)}, s32[512,1]{1,0:T(8,128)S(1)}, u32[]{:S(2)}) copy-start(s32[512,1]{1,0:T(8,128)S(1)} %copy.61.q_seg_ref) | copy-start | bytes 6148
  97.5 124.8 %collective-permute-start.2 = (bf16[512,1536]{1,0:T(8,128)(2,1)}, bf16[512,1536]{1,0:T(8,128)(2,1)}, u32[]{:S(2)}, u32[]{:S(2)}) collective-permute-start(bf16[512,1536]{1,0:T(8,128)(2,1)} %get-tuple-element.89), channel_id=1, source_target_pairs={{0,1},{2,3},{4,5},{6,7},{8,9},{10,11},{12,13},{14,15},{16,17},{18,... | collective-permute-start | bytes 4718600 | tf_op jit(solution)/shard_map/ppermute | solution.py:244
  107.5 50.1 %copy-start.14 = (bf16[512,768]{1,0:T(8,128)(2,1)}, bf16[512,768]{1,0:T(8,128)(2,1)S(1)}, u32[]{:S(2)}) copy-start(bf16[512,768]{1,0:T(8,128)(2,1)S(1)} %get-tuple-element.103.q_ref) | copy-start | bytes 2359300
  107.5 83.3 %copy-start.10 = (bf16[512,768]{1,0:T(8,128)(2,1)}, bf16[512,768]{1,0:T(8,128)(2,1)S(1)}, u32[]{:S(2)}) copy-start(bf16[512,768]{1,0:T(8,128)(2,1)S(1)} %get-tuple-element.102.q_ref) | copy-start | bytes 2359300
  107.6 116.3 %copy-start.8 = (bf16[512,768]{1,0:T(8,128)(2,1)}, bf16[512,768]{1,0:T(8,128)(2,1)S(1)}, u32[]{:S(2)}) copy-start(bf16[512,768]{1,0:T(8,128)(2,1)S(1)} %get-tuple-element.101.q_ref) | copy-start | bytes 2359300
  138.9 18.7 %copy-start.4 = (bf16[1024,768]{1,0:T(8,128)(2,1)}, bf16[1024,768]{1,0:T(8,128)(2,1)S(1)}, u32[]{:S(2)}) copy-start(bf16[1024,768]{1,0:T(8,128)(2,1)S(1)} %get-tuple-element.96.v_ref) | copy-start | bytes 4718596
  138.9 18.7 %copy-start.6 = (bf16[1024,768]{1,0:T(8,128)(2,1)}, bf16[1024,768]{1,0:T(8,128)(2,1)S(1)}, u32[]{:S(2)}) copy-start(bf16[1024,768]{1,0:T(8,128)(2,1)S(1)} %get-tuple-element.97.k_ref) | copy-start | bytes 4718596
  138.9 50.2 %copy-start.52 = (bf16[512,1536]{1,0:T(8,128)(2,1)S(1)}, bf16[512,1536]{1,0:T(8,128)(2,1)}, u32[]{:S(2)}) copy-start(bf16[512,1536]{1,0:T(8,128)(2,1)} %get-tuple-element.91) | copy-start | bytes 4718596
  157.6 33.2 %copy-start.34 = (f32[512,768]{1,0:T(8,128)}, f32[512,768]{1,0:T(8,128)S(1)}, u32[]{:S(2)}) copy-start(f32[512,768]{1,0:T(8,128)S(1)} %get-tuple-element.26.lse_ref) | copy-start | bytes 4718596
  157.6 51.7 %copy-start.24 = (bf16[512,768]{1,0:T(8,128)(2,1)}, bf16[512,768]{1,0:T(8,128)(2,1)S(1)}, u32[]{:S(2)}) copy-start(bf16[512,768]{1,0:T(8,128)(2,1)S(1)} %get-tuple-element.23.o_ref) | copy-start | bytes 2359300
  190.8 18.6 %copy-start = (bf16[1024,768]{1,0:T(8,128)(2,1)}, bf16[1024,768]{1,0:T(8,128)(2,1)S(1)}, u32[]{:S(2)}) copy-start(bf16[1024,768]{1,0:T(8,128)(2,1)S(1)} %get-tuple-element.94.v_ref) | copy-start | bytes 4718596
  190.8 18.6 %copy-start.2 = (bf16[1024,768]{1,0:T(8,128)(2,1)}, bf16[1024,768]{1,0:T(8,128)(2,1)S(1)}, u32[]{:S(2)}) copy-start(bf16[1024,768]{1,0:T(8,128)(2,1)S(1)} %get-tuple-element.95.k_ref) | copy-start | bytes 4718596
  190.8 31.4 %copy-start.51 = (bf16[512,1536]{1,0:T(8,128)(2,1)S(1)}, bf16[512,1536]{1,0:T(8,128)(2,1)}, u32[]{:S(2)}) copy-start(bf16[512,1536]{1,0:T(8,128)(2,1)} %get-tuple-element.89) | copy-start | bytes 4718596
  209.3 14.5 %copy-start.32 = (f32[512,768]{1,0:T(8,128)}, f32[512,768]{1,0:T(8,128)S(1)}, u32[]{:S(2)}) copy-start(f32[512,768]{1,0:T(8,128)S(1)} %get-tuple-element.28.lse_ref) | copy-start | bytes 4718596
  209.3 33.0 %copy-start.22 = (bf16[512,768]{1,0:T(8,128)(2,1)}, bf16[512,768]{1,0:T(8,128)(2,1)S(1)}, u32[]{:S(2)}) copy-start(bf16[512,768]{1,0:T(8,128)(2,1)S(1)} %get-tuple-element.24.o_ref) | copy-start | bytes 2359300
  250.5 72.6 %copy-start.67 = (f32[1536]{0:T(1024)}, f32[1536]{0:T(1024)S(1)}, u32[]{:S(2)}) copy-start(f32[1536]{0:T(1024)S(1)} %broadcast_multiply_fusion) | copy-start | bytes 18436
  253.3 69.8 %copy-start.74 = (f32[1536]{0:T(1024)}, f32[1536]{0:T(1024)S(1)}, u32[]{:S(2)}) copy-start(f32[1536]{0:T(1024)S(1)} %fusion.49) | copy-start | bytes 18436
  266.6 20.4 %copy-start.40 = (bf16[3,512,768]{2,1,0:T(8,128)(2,1)S(1)}, bf16[3,512,768]{2,1,0:T(8,128)(2,1)}, u32[]{:S(2)}) copy-start(bf16[3,512,768]{2,1,0:T(8,128)(2,1)} %param.17) | copy-start | bytes 7077892
  266.6 43.6 %slice-start = ((s8[4718592]{0:T(1024)(128)(4,1)}), s8[4194304]{0:T(1024)(128)(4,1)S(1)}, s32[]{:S(2)}) async-start(s8[4718592]{0:T(1024)(128)(4,1)} %bitcast.93), calls=%async_computation.6 | async-start | bytes 8388608
  287.0 23.2 %slice-start.1 = ((s8[4718592]{0:T(1024)(128)(4,1)}), s8[524288]{0:T(1024)(128)(4,1)S(1)}, s32[]{:S(2)}) async-start(s8[4718592]{0:T(1024)(128)(4,1)} %bitcast.93), calls=%async_computation.7 | async-start | bytes 1048576
  357.4 25.6 %copy-start.45 = (bf16[1024,1536]{1,0:T(8,128)(2,1)}, bf16[1024,1536]{1,0:T(8,128)(2,1)S(1)}, u32[]{:S(2)}) copy-start(bf16[1024,1536]{1,0:T(8,128)(2,1)S(1)} %constant_dynamic-update-slice_fusion.3) | copy-start | bytes 9437188
  358.6 60.8 %collective-permute-start.3 = (bf16[512,1536]{1,0:T(8,128)(2,1)}, bf16[512,1536]{1,0:T(8,128)(2,1)}, u32[]{:S(2)}, u32[]{:S(2)}) collective-permute-start(bf16[512,1536]{1,0:T(8,128)(2,1)} %slice.293), channel_id=1, source_target_pairs={{1,0},{3,2},{5,4},{7,6},{9,8},{11,10},{13,12},{15,14},{17,16},{19,... | collective-permute-start | bytes 4718600 | tf_op jit(solution)/shard_map/ppermute | solution.py:321
  384.6 66.3 %collective-permute-start.4 = (bf16[512,1536]{1,0:T(8,128)(2,1)}, bf16[512,1536]{1,0:T(8,128)(2,1)}, u32[]{:S(2)}, u32[]{:S(2)}) collective-permute-start(bf16[512,1536]{1,0:T(8,128)(2,1)} %slice.295), channel_id=1, source_target_pairs={{1,0},{3,2},{5,4},{7,6},{9,8},{11,10},{13,12},{15,14},{17,16},{19,... | collective-permute-start | bytes 4718600 | tf_op jit(solution)/shard_map/ppermute | solution.py:321
  408.0 11.4 %copy-start.46 = (bf16[1024,1536]{1,0:T(8,128)(2,1)S(1)}, bf16[1024,1536]{1,0:T(8,128)(2,1)}, u32[]{:S(2)}) copy-start(bf16[1024,1536]{1,0:T(8,128)(2,1)} %copy-done.45) | copy-start | bytes 9437188
  409.3 70.0 %collective-permute-start.5 = (bf16[512,1536]{1,0:T(8,128)(2,1)}, bf16[512,1536]{1,0:T(8,128)(2,1)}, u32[]{:S(2)}, u32[]{:S(2)}) collective-permute-start(bf16[512,1536]{1,0:T(8,128)(2,1)} %slice.297), channel_id=1, source_target_pairs={{1,0},{3,2},{5,4},{7,6},{9,8},{11,10},{13,12},{15,14},{17,16},{19,... | collective-permute-start | bytes 4718600 | tf_op jit(solution)/shard_map/ppermute | solution.py:321
  413.8 37.1 %copy-start.48 = (bf16[1024,1536]{1,0:T(8,128)(2,1)S(1)}, bf16[1024,1536]{1,0:T(8,128)(2,1)}, u32[]{:S(2)}) copy-start(bf16[1024,1536]{1,0:T(8,128)(2,1)} %copy-done.47) | copy-start | bytes 9437188
  419.4 60.0 %copy-start.50 = (bf16[1024,1536]{1,0:T(8,128)(2,1)S(1)}, bf16[1024,1536]{1,0:T(8,128)(2,1)}, u32[]{:S(2)}) copy-start(bf16[1024,1536]{1,0:T(8,128)(2,1)} %copy-done.49) | copy-start | bytes 9437188
  421.3 59.8 %copy-start.13 = (bf16[512,768]{1,0:T(8,128)(2,1)S(1)}, bf16[512,768]{1,0:T(8,128)(2,1)}, u32[]{:S(2)}) copy-start(bf16[512,768]{1,0:T(8,128)(2,1)} %copy-done.12) | copy-start | bytes 2359300
  421.3 59.8 %copy-start.17 = (bf16[512,768]{1,0:T(8,128)(2,1)S(1)}, bf16[512,768]{1,0:T(8,128)(2,1)}, u32[]{:S(2)}) copy-start(bf16[512,768]{1,0:T(8,128)(2,1)} %copy-done.16) | copy-start | bytes 2359300
  421.4 59.8 %copy-start.19 = (bf16[512,768]{1,0:T(8,128)(2,1)S(1)}, bf16[512,768]{1,0:T(8,128)(2,1)}, u32[]{:S(2)}) copy-start(bf16[512,768]{1,0:T(8,128)(2,1)} %copy-done.18) | copy-start | bytes 2359300
  528.7 11.1 %copy-start.58 = (bf16[768,768]{1,0:T(8,128)(2,1)S(1)}, bf16[768,768]{1,0:T(8,128)(2,1)}, u32[]{:S(2)}) copy-start(bf16[768,768]{1,0:T(8,128)(2,1)} %convolution_convert_fusion.5) | copy-start | bytes 3538948
  544.7 253.1 %reduce-scatter.5.cloned.1.call-start = ((), (), s32[]{:S(2)}) async-start(), calls=%async_computation.4 | async-start | bytes 9732096 | tf_op jit(solution)/shard_map/reduce_scatter | solution.py:208
  565.9 13.1 %copy-start.44 = (bf16[768,3072]{1,0:T(8,128)(2,1)S(1)}, bf16[768,3072]{1,0:T(8,128)(2,1)}, u32[]{:S(2)}) copy-start(bf16[768,3072]{1,0:T(8,128)(2,1)} %reshape.198) | copy-start | bytes 14155780
  583.8 13.4 %copy-start.76 = (f32[1536]{0:T(1024)S(1)}, f32[1536]{0:T(1024)}, u32[]{:S(2)}) copy-start(f32[1536]{0:T(1024)} %get-tuple-element.73) | copy-start | bytes 18436
  583.8 13.4 %copy-start.41 = (bf16[3,512,768]{2,1,0:T(8,128)(2,1)S(1)}, bf16[3,512,768]{2,1,0:T(8,128)(2,1)}, u32[]{:S(2)}) copy-start(bf16[3,512,768]{2,1,0:T(8,128)(2,1)} %param.17) | copy-start | bytes 7077892
  583.8 13.4 %copy-start.64 = (f32[1536]{0:T(1024)S(1)}, f32[1536]{0:T(1024)}, u32[]{:S(2)}) copy-start(f32[1536]{0:T(1024)} %copy-done.63) | copy-start | bytes 18436
  583.8 13.5 %copy-start.66 = (f32[1536]{0:T(1024)S(1)}, f32[1536]{0:T(1024)}, u32[]{:S(2)}) copy-start(f32[1536]{0:T(1024)} %copy-done.65) | copy-start | bytes 18436
  583.8 13.5 %copy-start.73 = (f32[768]{0:T(1024)S(1)}, f32[768]{0:T(1024)}, u32[]{:S(2)}) copy-start(f32[768]{0:T(1024)} %copy-done.71) | copy-start | bytes 9220
  (49 other events, 202.7 us)
Sparse Core Ops, SparseCore 0:
  11.5 63.4 all-gather.2
  77.9 98.0 all-gather.4
  544.8 111.5 reduce-scatter.6
  663.1 134.5 reduce-scatter.4
